TPU v7x, 32 devices: a whole 2x2x4 slice. The times are simulated.
32 devices in a mesh: dp: 8 (over z, y), tensor: 4 (over x, core).
Axes of the slice: x: 2, y: 2, z: 4, core: 2. Of those that a mesh axis runs over, the one named last changes fastest.
Arguments:
- hidden: float32 [12288, 768], P(('dp', 'tensor')), may hold values from -6 to 6
- segments: int32 [12288], P('dp'), may hold values from 0 to 512, as said below
- w_qkv: bfloat16 [2, 768, 2304], P(None, 'dp', 'tensor'), may hold values from -0.21875 to 0.21875
- w_out: bfloat16 [2, 768, 768], P(None, 'dp', 'tensor'), may hold values from -0.875 to 0.875
- w_up: bfloat16 [2, 768, 3072], P(None, 'dp', 'tensor'), may hold values from -0.21875 to 0.21875
- w_down: bfloat16 [2, 768, 3072], P(None, 'dp', 'tensor'), may hold values from -0.109375 to 0.109375
- ln_gain: float32 [2, 2, 768], replicated, may hold values from 0.5 to 1.5
- ln_bias: float32 [2, 2, 768], replicated, may hold values from -1.8 to 1.8
- branch_bias: float32 [2, 768], replicated, may hold values from -1.8 to 1.8
- qkv_bias: float32 [2, 2304], replicated, may hold values from -1.8 to 1.8
- up_bias: float32 [2, 3072], replicated, may hold values from -1.8 to 1.8
- cotangent: float32 [12288, 768], P(('dp', 'tensor')), may hold values from -6 to 6
Outputs:
- hidden_out: float32 [12288, 768], P(('dp', 'tensor'))
- hidden_grad: float32 [12288, 768], P(('dp', 'tensor'))
- w_qkv_grad: float32 [2, 768, 2304], P(None, 'dp', 'tensor')
- w_out_grad: float32 [2, 768, 768], P(None, 'dp', 'tensor')
- w_up_grad: float32 [2, 768, 3072], P(None, 'dp', 'tensor')
- w_down_grad: float32 [2, 768, 3072], P(None, 'dp', 'tensor')
- ln_gain_grad: float32 [2, 2, 768], replicated
- ln_bias_grad: float32 [2, 2, 768], replicated
- branch_bias_grad: float32 [2, 768], replicated
- qkv_bias_grad: float32 [2, 2304], replicated
- up_bias_grad: float32 [2, 3072], replicated
Inputs may be any that keep to these rules, and one draw needn't show every extreme that they name: `segments`: within each group of 1536 consecutive tokens the ids start at 0 and rise by one where a new sequence begins; every sequence has at most 1024 tokens, and each group holds one of exactly 1024.
All inputs are finite; a program needn't handle non-finite values.
Results may differ from a plain program's by a relative error of at most 0.018.
Values may be sent and summed in bfloat16 or wider, within the bound.
A program may use at most 192 MiB of HBM per device.

v0:
```python
import math

import jax
import jax.numpy as jnp
from jax import lax
from jax.sharding import PartitionSpec as P

D = 768
HEADS = 12
HEAD_DIM = 64
FF = 3072
ROT = 16
LAYERS = 2


NORM_EPS = 1e-05
MASKED = -1e30


def layer_norm(values_in, gain, shift):
    average = jnp.mean(values_in, axis=-1, keepdims=True)
    centered = values_in - average
    variance = jnp.mean(centered * centered, axis=-1, keepdims=True)
    return centered * lax.rsqrt(variance + NORM_EPS) * gain + shift


def both_norms(values_in, gain_one, shift_one, gain_two, shift_two):
    return (layer_norm(values_in, gain_one, shift_one), layer_norm(values_in, gain_two, shift_two))


def positions(seg_group):
    places = jnp.arange(seg_group.shape[0], dtype=jnp.int32)
    fresh = jnp.concatenate([jnp.ones((1,), dtype=bool), seg_group[1:] != seg_group[:-1]])
    starts = lax.cummax(jnp.where(fresh, places, 0), axis=0)
    return places - starts


def rotary_tables(token_place):
    half_rot = ROT // 2
    exponent = jnp.arange(half_rot, dtype=jnp.float32) * (-2.0 * math.log(10000.0) / ROT)
    angles = token_place.astype(jnp.float32)[:, None] * jnp.exp(exponent)[None, :]
    return (jnp.cos(angles), jnp.sin(angles))


def rotate_heads(heads, cosine, sine_table):
    half_rot = ROT // 2
    first_half = heads[..., :half_rot]
    second_half = heads[..., half_rot:ROT]
    cos_wide = cosine[:, None, :]
    sin_wide = sine_table[:, None, :]
    return jnp.concatenate(
        [
            first_half * cos_wide - second_half * sin_wide,
            second_half * cos_wide + first_half * sin_wide,
            heads[..., ROT:],
        ],
        axis=-1,
    )


def against(left, right):
    return lax.dot_general(
        left, right, (((1,), (1,)), ((), ())), preferred_element_type=jnp.float32
    )


def over_rows(left, right):
    return lax.dot_general(
        left, right, (((0,), (0,)), ((), ())), preferred_element_type=jnp.float32
    )


def placed(local_part, full_width, tensor_rank):
    empty = jnp.zeros((full_width,), jnp.float32)
    return lax.dynamic_update_slice_in_dim(empty, local_part, tensor_rank * local_part.shape[0], 0)


def block_scores(query_heads, key_heads, seg_group, first_row, block_rows, score_scale):
    places = jnp.arange(seg_group.shape[0], dtype=jnp.int32)
    rows_here = first_row + jnp.arange(block_rows, dtype=jnp.int32)
    seg_here = lax.dynamic_slice_in_dim(seg_group, first_row, block_rows, 0)
    allowed = (seg_here[:, None] == seg_group[None, :]) & (places[None, :] <= rows_here[:, None])
    query_block = lax.dynamic_slice_in_dim(query_heads, first_row, block_rows, 0)
    scores = (
        jnp.einsum("qhd,khd->hqk", query_block, key_heads, preferred_element_type=jnp.float32)
        * score_scale
    )
    return (query_block, jnp.where(allowed[None], scores, MASKED))


def attention_forward(query_heads, key_heads, value_heads, seg_group, score_scale):
    group_rows = seg_group.shape[0]
    block_rows = min(512, group_rows)

    def one_block(first_row):
        query_block, scores = block_scores(
            query_heads, key_heads, seg_group, first_row, block_rows, score_scale
        )
        row_max = jnp.max(scores, axis=-1, keepdims=True)
        exp_scores = jnp.exp(scores - row_max)
        exp_total = jnp.sum(exp_scores, axis=-1, keepdims=True)
        prob_low = (exp_scores / exp_total).astype(jnp.bfloat16)
        context = jnp.einsum(
            "hqk,khd->qhd", prob_low, value_heads, preferred_element_type=jnp.float32
        )
        return (context.astype(jnp.bfloat16), (row_max + jnp.log(exp_total))[..., 0])

    first_rows = jnp.arange(group_rows // block_rows, dtype=jnp.int32) * block_rows
    context, logsum = lax.map(one_block, first_rows)
    return (context.reshape(query_heads.shape), logsum)


def attention_backward(
    query_heads, key_heads, value_heads, seg_group, logsum, grad_context, score_scale
):
    group_rows = seg_group.shape[0]
    block_rows = min(512, group_rows)

    def one_block(carry, member):
        key_grad, value_grad = carry
        first_row, block_logsum = member
        query_block, scores = block_scores(
            query_heads, key_heads, seg_group, first_row, block_rows, score_scale
        )
        prob_full = jnp.exp(scores - block_logsum[..., None])
        grad_block = lax.dynamic_slice_in_dim(grad_context, first_row, block_rows, 0)
        value_grad = value_grad + jnp.einsum(
            "hqk,qhd->khd",
            prob_full.astype(jnp.bfloat16),
            grad_block,
            preferred_element_type=jnp.float32,
        )
        grad_prob = jnp.einsum(
            "qhd,khd->hqk", grad_block, value_heads, preferred_element_type=jnp.float32
        )
        inner_sum = jnp.sum(prob_full * grad_prob, axis=-1, keepdims=True)
        grad_scores = (prob_full * (grad_prob - inner_sum)).astype(jnp.bfloat16)
        query_grad = (
            jnp.einsum("hqk,khd->qhd", grad_scores, key_heads, preferred_element_type=jnp.float32)
            * score_scale
        )
        key_grad = (
            key_grad
            + jnp.einsum(
                "hqk,qhd->khd", grad_scores, query_block, preferred_element_type=jnp.float32
            )
            * score_scale
        )
        return ((key_grad, value_grad), query_grad)

    first_rows = jnp.arange(group_rows // block_rows, dtype=jnp.int32) * block_rows
    zero_grad = jnp.zeros(key_heads.shape, jnp.float32)
    carried, query_grad = lax.scan(one_block, (zero_grad, zero_grad), (first_rows, logsum))
    return (query_grad.reshape(key_heads.shape), carried[0], carried[1])


def local(
    hidden,
    segments,
    w_qkv,
    w_out,
    w_up,
    w_down,
    ln_gain,
    ln_bias,
    branch_bias,
    qkv_bias,
    up_bias,
    cotangent,
):
    tensor_rank = lax.axis_index("tensor")
    local_heads = HEADS // lax.axis_size("tensor")
    width_qkv = w_qkv.shape[2]
    width_up = w_up.shape[2]
    group_rows = segments.shape[0]
    score_scale = HEAD_DIM ** (-0.5)
    cosine, sine_table = rotary_tables(positions(segments))
    stored = []
    fetched = []
    for which_layer in range(LAYERS):
        qkv_full, out_full, up_full, down_full = (
            lax.all_gather(w_qkv[which_layer], "dp", axis=0, tiled=True),
            lax.all_gather(w_out[which_layer], "dp", axis=0, tiled=True),
            lax.all_gather(w_up[which_layer], "dp", axis=0, tiled=True),
            lax.all_gather(w_down[which_layer], "dp", axis=0, tiled=True),
        )
        normed_one = layer_norm(hidden, ln_gain[which_layer, 0], ln_bias[which_layer, 0]).astype(
            jnp.bfloat16
        )
        normed_two = layer_norm(hidden, ln_gain[which_layer, 1], ln_bias[which_layer, 1]).astype(
            jnp.bfloat16
        )
        rows_one, rows_two = (
            lax.all_gather(normed_one, "tensor", axis=0, tiled=True),
            lax.all_gather(normed_two, "tensor", axis=0, tiled=True),
        )
        qkv_here = lax.dynamic_slice_in_dim(
            qkv_bias[which_layer], tensor_rank * width_qkv, width_qkv
        )
        mixed_cols = jnp.dot(rows_one, qkv_full, preferred_element_type=jnp.float32) + qkv_here
        mixed_cols = mixed_cols.reshape(group_rows, local_heads, 3, HEAD_DIM)
        query_heads = rotate_heads(mixed_cols[:, :, 0], cosine, sine_table).astype(jnp.bfloat16)
        key_heads = rotate_heads(mixed_cols[:, :, 1], cosine, sine_table).astype(jnp.bfloat16)
        value_heads = mixed_cols[:, :, 2].astype(jnp.bfloat16)
        context, logsum = attention_forward(
            query_heads, key_heads, value_heads, segments, score_scale
        )
        flat_context = context.reshape(group_rows, local_heads * HEAD_DIM)
        up_here = lax.dynamic_slice_in_dim(up_bias[which_layer], tensor_rank * width_up, width_up)
        up_proj = jnp.dot(rows_two, up_full, preferred_element_type=jnp.float32) + up_here
        activated = jax.nn.gelu(up_proj, approximate=False).astype(jnp.bfloat16)
        branch = (
            lax.psum_scatter(
                (against(flat_context, out_full) + against(activated, down_full)).astype(
                    jnp.bfloat16
                ),
                "tensor",
                scatter_dimension=0,
                tiled=True,
            ).astype(jnp.float32)
            + branch_bias[which_layer]
        )
        stored.append(
            (
                hidden,
                rows_one,
                rows_two,
                query_heads,
                key_heads,
                value_heads,
                flat_context,
                logsum,
                up_proj,
                activated,
            )
        )
        fetched.append((qkv_full, out_full, up_full, down_full))
        hidden = hidden + branch
    grad_hidden = cotangent
    weight_parts = [None] * LAYERS
    small_parts = [None] * LAYERS
    inverse_root = 1.0 / math.sqrt(2.0)
    density = 1.0 / math.sqrt(2.0 * math.pi)
    for which_layer in reversed(range(LAYERS)):
        (
            layer_input,
            rows_one,
            rows_two,
            query_heads,
            key_heads,
            value_heads,
            flat_context,
            logsum,
            up_proj,
            activated,
        ) = stored[which_layer]
        qkv_full, out_full, up_full, down_full = (
            lax.all_gather(w_qkv[which_layer], "dp", axis=0, tiled=True),
            lax.all_gather(w_out[which_layer], "dp", axis=0, tiled=True),
            lax.all_gather(w_up[which_layer], "dp", axis=0, tiled=True),
            lax.all_gather(w_down[which_layer], "dp", axis=0, tiled=True),
        )
        grad_branch = grad_hidden.astype(jnp.bfloat16)
        branch_sum = jnp.sum(grad_branch.astype(jnp.float32), axis=0)
        grad_gathered = lax.all_gather(grad_branch, "tensor", axis=0, tiled=True)
        out_grad = over_rows(grad_gathered, flat_context)
        down_grad = over_rows(grad_gathered, activated)
        grad_context = jnp.dot(grad_gathered, out_full, preferred_element_type=jnp.float32).astype(
            jnp.bfloat16
        )
        grad_context = grad_context.reshape(group_rows, local_heads, HEAD_DIM)
        grad_act = jnp.dot(grad_gathered, down_full, preferred_element_type=jnp.float32)
        normal_cdf = 0.5 * (1.0 + lax.erf(up_proj * inverse_root))
        slope = normal_cdf + up_proj * jnp.exp(-0.5 * up_proj * up_proj) * density
        grad_up = (grad_act * slope).astype(jnp.bfloat16)
        up_grad = over_rows(rows_two, grad_up)
        up_bias_part = jnp.sum(grad_up.astype(jnp.float32), axis=0)
        query_grad, key_grad, value_grad = attention_backward(
            query_heads, key_heads, value_heads, segments, logsum, grad_context, score_scale
        )
        query_grad = rotate_heads(query_grad, cosine, -sine_table)
        key_grad = rotate_heads(key_grad, cosine, -sine_table)
        grad_mixed = (
            jnp.stack([query_grad, key_grad, value_grad], axis=2)
            .reshape(group_rows, width_qkv)
            .astype(jnp.bfloat16)
        )
        qkv_grad = over_rows(rows_one, grad_mixed)
        qkv_bias_part = jnp.sum(grad_mixed.astype(jnp.float32), axis=0)
        gain_first = ln_gain[which_layer, 0]
        gain_second = ln_gain[which_layer, 1]
        grad_normed = lax.psum_scatter(
            jnp.concatenate(
                [against(grad_mixed, qkv_full), against(grad_up, up_full)], axis=1
            ).astype(jnp.bfloat16),
            "tensor",
            scatter_dimension=0,
            tiled=True,
        ).astype(jnp.float32)
        ignored, norm_pull = jax.vjp(
            both_norms,
            layer_input,
            gain_first,
            ln_bias[which_layer, 0],
            gain_second,
            ln_bias[which_layer, 1],
        )
        input_grad, gain_one, shift_one, gain_two, shift_two = norm_pull(
            (grad_normed[:, :D], grad_normed[:, D:])
        )
        grad_hidden = grad_hidden + input_grad
        weight_parts[which_layer] = (
            lax.psum_scatter(qkv_grad, "dp", scatter_dimension=0, tiled=True),
            lax.psum_scatter(out_grad, "dp", scatter_dimension=0, tiled=True),
            lax.psum_scatter(up_grad, "dp", scatter_dimension=0, tiled=True),
            lax.psum_scatter(down_grad, "dp", scatter_dimension=0, tiled=True),
        )
        small_parts[which_layer] = (
            jnp.stack([gain_one, gain_two]),
            jnp.stack([shift_one, shift_two]),
            branch_sum,
            placed(qkv_bias_part, 3 * D, tensor_rank),
            placed(up_bias_part, FF, tensor_rank),
        )
    gain_stack = jnp.stack([small_parts[which_layer][0] for which_layer in range(LAYERS)])
    shift_stack = jnp.stack([small_parts[which_layer][1] for which_layer in range(LAYERS)])
    branch_stack = jnp.stack([small_parts[which_layer][2] for which_layer in range(LAYERS)])
    qkv_stack = jnp.stack([small_parts[which_layer][3] for which_layer in range(LAYERS)])
    up_stack = jnp.stack([small_parts[which_layer][4] for which_layer in range(LAYERS)])
    gain_total, shift_total, branch_total, qkv_total, up_total = lax.psum(
        (gain_stack, shift_stack, branch_stack, qkv_stack, up_stack), ("dp", "tensor")
    )
    qkv_weights = jnp.stack([weight_parts[which_layer][0] for which_layer in range(LAYERS)])
    out_weights = jnp.stack([weight_parts[which_layer][1] for which_layer in range(LAYERS)])
    up_weights = jnp.stack([weight_parts[which_layer][2] for which_layer in range(LAYERS)])
    down_weights = jnp.stack([weight_parts[which_layer][3] for which_layer in range(LAYERS)])
    return (
        hidden,
        grad_hidden,
        qkv_weights,
        out_weights,
        up_weights,
        down_weights,
        gain_total,
        shift_total,
        branch_total,
        qkv_total,
        up_total,
    )


def solution(mesh):
    return jax.shard_map(
        local,
        mesh=mesh,
        in_specs=(
            P(("dp", "tensor"), None),
            P("dp"),
            P(None, "dp", "tensor"),
            P(None, "dp", "tensor"),
            P(None, "dp", "tensor"),
            P(None, "dp", "tensor"),
            P(),
            P(),
            P(),
            P(),
            P(),
            P(("dp", "tensor"), None),
        ),
        out_specs=(
            P(("dp", "tensor"), None),
            P(("dp", "tensor"), None),
            P(None, "dp", "tensor"),
            P(None, "dp", "tensor"),
            P(None, "dp", "tensor"),
            P(None, "dp", "tensor"),
            P(),
            P(),
            P(),
            P(),
            P(),
        ),
        check_vma=False,
    )
```

profile of v0, /device:TPU:0, one launch (start us, length us, event | category | flops | bytes accessed | tf_op | source)
XLA Modules:
  0.0 1353.1 jit_solution(2115944990441068203)
XLA Ops:
  18.9 35.1 %all-gather.1 = bf16[1,768,192]{2,1,0:T(8,128)(2,1)} all-gather(bf16[1,96,192]{2,1,0:T(8,128)(2,1)S(1)} %get-tuple-element.475), channel_id=3, replica_groups=mesh['dp'=8,'tensor'=4] {'dp'}, dimensions={1}, use_global_device_ids=true | all-gather | bytes 331776 | tf_op jit(solution)/shard_map/all_gather | solution.py:183
  54.0 35.0 %all-gather = bf16[1,768,576]{2,1,0:T(8,128)(2,1)S(1)} all-gather(bf16[1,96,576]{2,1,0:T(8,128)(2,1)S(1)} %get-tuple-element.469), channel_id=2, replica_groups=mesh['dp'=8,'tensor'=4] {'dp'}, dimensions={1}, use_global_device_ids=true | all-gather | bytes 995328 | tf_op jit(solution)/shard_map/all_gather | solution.py:182
  94.8 40.4 %while.54 = (s32[]{:T(128)}, bf16[3,512,3,64]{1,3,2,0:T(8,128)(2,1)S(1)}, f32[3,3,512]{2,1,0:T(4,128)}, s32[3]{0:T(128)S(1)}, s32[1536]{0:T(1024)S(1)}, /*index=...) while((s32[]{:T(128)}, ...), condition=%wide.region_7.8_spmd, body=%wide.region_4.0_spmd.sunk | while | flops 634747904 | bytes 33102008 | solution.py:109
  135.9 14.8 %fusion.68 = (bf16[1536,768]{1,0:T(8,128)(2,1)}, f32[1536,768]{1,0:T(8,128)}) fusion(f32[768]{0:T(1024)S(1)} %dynamic-slice_reduce_fusion.1, bf16[1536,768]{1,0:T(8,128)(2,1)} %all-gather.21.cloned.1.call-done, bf16[1,768,768]{2,1,0:T(8,128)(2,1)} %all-gather.31.cloned.1.call-done), kind=kOutput, calls=%fused_computation.92 | convolution fusion | flops 1889796096 | bytes 10619904 | tf_op jit(solution)/shard_map/dot_general | solution.py:210
  169.2 28.5 %reduce-scatter.13.cloned.1.call-done = bf16[384,768]{1,0:T(8,128)(2,1)} async-done(((bf16[1536,768]{1,0:T(8,128)(2,1)}), bf16[384,768]{1,0:T(8,128)(2,1)}) %reduce-scatter.13.cloned.1.call-update) | async-done | bytes 589840 | tf_op jit(solution)/shard_map/reduce_scatter | solution.py:213
  205.7 31.2 %all-gather.5 = bf16[1,768,192]{2,1,0:T(8,128)(2,1)S(1)} all-gather(bf16[1,96,192]{2,1,0:T(8,128)(2,1)S(1)} %copy-done.51), channel_id=7, replica_groups=mesh['dp'=8,'tensor'=4] {'dp'}, dimensions={1}, use_global_device_ids=true | all-gather | bytes 331776 | tf_op jit(solution)/shard_map/all_gather | solution.py:183
  236.9 35.2 %all-gather.4 = bf16[1,768,576]{2,1,0:T(8,128)(2,1)} all-gather(bf16[1,96,576]{2,1,0:T(8,128)(2,1)S(1)} %copy-done.43), channel_id=6, replica_groups=mesh['dp'=8,'tensor'=4] {'dp'}, dimensions={1}, use_global_device_ids=true | all-gather | bytes 995328 | tf_op jit(solution)/shard_map/all_gather | solution.py:182
  282.9 42.7 %while.55 = (s32[]{:T(128)}, bf16[3,512,3,64]{1,3,2,0:T(8,128)(2,1)}, f32[3,3,512]{2,1,0:T(4,128)S(1)}, s32[3]{0:T(128)S(1)}, s32[1536]{0:T(1024)S(1)}, /*index=...) while((s32[]{:T(128)}, ...), condition=%wide.region_14.15_spmd, body=%wide.region_11.14_spmd.sunk | while | flops 634747904 | bytes 35461332 | solution.py:109
  327.1 125.7 %while.56 = (s32[]{:T(128)}, f32[1536,3,64]{0,2,1:T(8,128)S(1)}, f32[1536,3,64]{0,2,1:T(8,128)S(1)}, f32[3,512,3,64]{1,0,3,2:T(4,128)}, s32[3]{0:T(128)S(1)}, /*...) while((s32[]{:T(128)}, f32[1536,3,64]{0,2,1:T(8,128)S(1)}, ...), condition=%wide.region_18.19_spmd.clone, body=%wide.region_16.18_spmd.clone.sunk | while | flops 1535114240 | bytes 138262816 | solution.py:153
  464.2 14.8 %fusion.71 = (bf16[1536,768]{1,0:T(8,128)(2,1)}, f32[1536,768]{1,0:T(8,128)}) fusion(f32[768]{0:T(1024)S(1)} %copy-done.90, bf16[1536,768]{1,0:T(8,128)(2,1)} %all-gather.25.cloned.1.call-done, bf16[1,768,768]{2,1,0:T(8,128)(2,1)} %all-gather.35.cloned.1.call-done), kind=kOutput, calls=%fused_computation.95 | convolution fusion | flops 1889796096 | bytes 10619904 | tf_op jit(solution)/shard_map/dot_general | solution.py:210
  499.3 41.0 %reduce-scatter.17.cloned.1.call-done = bf16[384,1536]{1,0:T(8,128)(2,1)} async-done(((bf16[1536,1536]{1,0:T(8,128)(2,1)}), bf16[384,1536]{1,0:T(8,128)(2,1)}) %reduce-scatter.17.cloned.1.call-update) | async-done | bytes 1179664 | tf_op jit(solution)/shard_map/reduce_scatter | solution.py:292
  544.5 31.3 %reduce-scatter.15.cloned.1.call-done = bf16[384,768]{1,0:T(8,128)(2,1)} async-done(((bf16[1536,768]{1,0:T(8,128)(2,1)}), bf16[384,768]{1,0:T(8,128)(2,1)}) %reduce-scatter.15.cloned.1.call-update) | async-done | bytes 589840 | tf_op jit(solution)/shard_map/reduce_scatter | solution.py:213
  583.2 21.9 %all-gather.29.cloned.1.call-done = bf16[1536,768]{1,0:T(8,128)(2,1)} async-done(((bf16[384,768]{1,0:T(8,128)(2,1)}), bf16[1536,768]{1,0:T(8,128)(2,1)}) %all-gather.29.cloned.1.call-update) | async-done | bytes 2359312 | tf_op jit(solution)/shard_map/all_gather | solution.py:265
  619.5 127.0 %while.57 = (s32[]{:T(128)}, f32[1536,3,64]{0,2,1:T(8,128)S(1)}, f32[1536,3,64]{0,2,1:T(8,128)S(1)}, f32[3,512,3,64]{1,0,3,2:T(4,128)}, s32[3]{0:T(128)S(1)}, /*...) while((s32[]{:T(128)}, f32[1536,3,64]{0,2,1:T(8,128)S(1)}, ...), condition=%wide.region_26.27_spmd.clone, body=%wide.region_24.26_spmd.clone.sunk | while | flops 1535114240 | bytes 138262816 | solution.py:153
  634.5 9.6 multiply_convert_fusion.5
  676.9 9.5 multiply_convert_fusion.5
  719.1 9.5 multiply_convert_fusion.5
  805.5 69.1 %reduce-scatter.21.cloned.1.call-done = f32[96,576]{1,0:T(8,128)} async-done(((f32[768,576]{1,0:T(8,128)}), f32[96,576]{1,0:T(8,128)}) %reduce-scatter.21.cloned.1.call-update) | async-done | bytes 221200 | tf_op jit(solution)/shard_map/reduce_scatter | solution.py:313
  876.5 69.9 %reduce-scatter.35.cloned.1.call-done = f32[96,768]{1,0:T(8,128)} async-done(((f32[768,768]{1,0:T(8,128)}), f32[96,768]{1,0:T(8,128)}) %reduce-scatter.35.cloned.1.call-update) | async-done | bytes 294928 | tf_op jit(solution)/shard_map/reduce_scatter | solution.py:316
  946.3 71.9 %reduce-scatter.33.cloned.1.call-done = f32[96,768]{1,0:T(8,128)} async-done(((f32[768,768]{1,0:T(8,128)}), f32[96,768]{1,0:T(8,128)}) %reduce-scatter.33.cloned.1.call-update) | async-done | bytes 294928 | tf_op jit(solution)/shard_map/reduce_scatter | solution.py:316
  1020.2 69.9 %reduce-scatter.31.cloned.1.call-done = f32[96,768]{1,0:T(8,128)} async-done(((f32[768,768]{1,0:T(8,128)}), f32[96,768]{1,0:T(8,128)}) %reduce-scatter.31.cloned.1.call-update) | async-done | bytes 294928 | tf_op jit(solution)/shard_map/reduce_scatter | solution.py:315
  1090.1 72.0 %reduce-scatter.29.cloned.1.call-done = f32[96,768]{1,0:T(8,128)} async-done(((f32[768,768]{1,0:T(8,128)}), f32[96,768]{1,0:T(8,128)}) %reduce-scatter.29.cloned.1.call-update) | async-done | bytes 294928 | tf_op jit(solution)/shard_map/reduce_scatter | solution.py:315
  1164.1 47.6 %reduce-scatter.19.cloned.1.call-done = bf16[384,1536]{1,0:T(8,128)(2,1)} async-done(((bf16[1536,1536]{1,0:T(8,128)(2,1)}), bf16[384,1536]{1,0:T(8,128)(2,1)}) %reduce-scatter.19.cloned.1.call-update) | async-done | bytes 1179664 | tf_op jit(solution)/shard_map/reduce_scatter | solution.py:292
  1219.0 120.8 %all-reduce.3.cloned.1.call-done = (f32[2,2,768]{2,1,0:T(2,128)}, f32[2,2,768]{2,1,0:T(2,128)}, f32[2,768]{1,0:T(2,128)}, f32[2,2304]{1,0:T(2,128)}, f32[2,3072]{1,0:T(2,128)}) async-done(((f32[2,2,768]{2,1,0:T(2,128)}, f32[2,2,768]{2,1,0:T(2,128)}, f32[2,768]{1,0:T(2,128)}, f32[2,2304]{1,0:T(2,128)}, f32[2,3072]{1,0:T(2,128)}), (f32[2,2,768]{2,1,0:T(2,128)}, f32[2,2,768]{2,1,0:T(2,128)}, ...) | async-done | bytes 73744 | tf_op jit(solution)/shard_map/psum | solution.py:330
  (554 shorter events, 474.6 us)
Async XLA Ops:
  7.2 82.8 %all-gather.19.cloned.1.call-start = ((), (), s32[]{:S(2)}) async-start(), calls=%async_computation.12 | async-start | bytes 2949120 | tf_op jit(solution)/shard_map/all_gather | solution.py:194
  13.1 122.8 %all-gather.31.cloned.1.call-start = ((), (), s32[]{:S(2)}) async-start(), calls=%async_computation.30 | async-start | bytes 1327104 | tf_op jit(solution)/shard_map/all_gather | solution.py:184
  13.9 122.0 %all-gather.21.cloned.1.call-start = ((), (), s32[]{:S(2)}) async-start(), calls=%async_computation.13 | async-start | bytes 2949120 | tf_op jit(solution)/shard_map/all_gather | solution.py:195
  14.7 144.6 %all-gather.33.cloned.1.call-start = ((), (), s32[]{:S(2)}) async-start(), calls=%async_computation.31 | async-start | bytes 1327104 | tf_op jit(solution)/shard_map/all_gather | solution.py:185
  15.5 182.2 %reduce-scatter.13.cloned.1.call-start = ((), (), s32[]{:S(2)}) async-start(), calls=%async_computation.14 | async-start | bytes 2949120 | tf_op jit(solution)/shard_map/reduce_scatter | solution.py:213
  165.8 106.3 %all-gather.27.cloned.1.call-start = ((), (), s32[]{:S(2)}) async-start(), calls=%async_computation.18 | async-start | bytes 2949120 | tf_op jit(solution)/shard_map/all_gather | solution.py:265
  168.5 107.0 %all-gather.23.cloned.1.call-start = ((), (), s32[]{:S(2)}) async-start(), calls=%async_computation.15 | async-start | bytes 2949120 | tf_op jit(solution)/shard_map/all_gather | solution.py:194
  199.3 72.7 %copy-start.73 = (f32[384]{0:T(512)}, f32[384]{0:T(512)S(1)}, u32[]{:S(2)}) copy-start(f32[384]{0:T(512)S(1)} %multiply_reduce_fusion.10) | copy-start | bytes 4612
  201.5 262.7 %all-gather.35.cloned.1.call-start = ((), (), s32[]{:S(2)}) async-start(), calls=%async_computation.32 | async-start | bytes 1327104 | tf_op jit(solution)/shard_map/all_gather | solution.py:184
  202.2 261.9 %all-gather.25.cloned.1.call-start = ((), (), s32[]{:S(2)}) async-start(), calls=%async_computation.16 | async-start | bytes 2949120 | tf_op jit(solution)/shard_map/all_gather | solution.py:195
  203.0 276.0 %all-gather.37.cloned.1.call-start = ((), (), s32[]{:S(2)}) async-start(), calls=%async_computation.33 | async-start | bytes 1327104 | tf_op jit(solution)/shard_map/all_gather | solution.py:185
  203.6 336.7 %reduce-scatter.17.cloned.1.call-start = ((), (), s32[]{:S(2)}) async-start(), calls=%async_computation.19 | async-start | bytes 5898240 | tf_op jit(solution)/shard_map/reduce_scatter | solution.py:292
  491.1 84.6 %reduce-scatter.15.cloned.1.call-start = ((), (), s32[]{:S(2)}) async-start(), calls=%async_computation.17 | async-start | bytes 2949120 | tf_op jit(solution)/shard_map/reduce_scatter | solution.py:213
  499.2 105.9 %all-gather.29.cloned.1.call-start = ((), (), s32[]{:S(2)}) async-start(), calls=%async_computation.20 | async-start | bytes 2949120 | tf_op jit(solution)/shard_map/all_gather | solution.py:265
  580.9 220.2 %reduce-scatter.27.cloned.1.call-start = ((), (), s32[]{:S(2)}) async-start(), calls=%async_computation.25 | async-start | bytes 884736 | tf_op jit(solution)/shard_map/reduce_scatter | solution.py:314
  583.2 218.0 %reduce-scatter.25.cloned.1.call-start = ((), (), s32[]{:S(2)}) async-start(), calls=%async_computation.24 | async-start | bytes 884736 | tf_op jit(solution)/shard_map/reduce_scatter | solution.py:314
  608.5 197.0 %reduce-scatter.23.cloned.1.call-start = ((), (), s32[]{:S(2)}) async-start(), calls=%async_computation.23 | async-start | bytes 2211840 | tf_op jit(solution)/shard_map/reduce_scatter | solution.py:313
  614.2 260.4 %reduce-scatter.21.cloned.1.call-start = ((), (), s32[]{:S(2)}) async-start(), calls=%async_computation.22 | async-start | bytes 2211840 | tf_op jit(solution)/shard_map/reduce_scatter | solution.py:313
  757.8 188.5 %reduce-scatter.35.cloned.1.call-start = ((), (), s32[]{:S(2)}) async-start(), calls=%async_computation.29 | async-start | bytes 2654208 | tf_op jit(solution)/shard_map/reduce_scatter | solution.py:316
  763.2 255.0 %reduce-scatter.33.cloned.1.call-start = ((), (), s32[]{:S(2)}) async-start(), calls=%async_computation.28 | async-start | bytes 2654208 | tf_op jit(solution)/shard_map/reduce_scatter | solution.py:316
  770.1 320.0 %reduce-scatter.31.cloned.1.call-start = ((), (), s32[]{:S(2)}) async-start(), calls=%async_computation.27 | async-start | bytes 2654208 | tf_op jit(solution)/shard_map/reduce_scatter | solution.py:315
  776.1 386.0 %reduce-scatter.29.cloned.1.call-start = ((), (), s32[]{:S(2)}) async-start(), calls=%async_computation.26 | async-start | bytes 2654208 | tf_op jit(solution)/shard_map/reduce_scatter | solution.py:315
  787.3 424.4 %reduce-scatter.19.cloned.1.call-start = ((), (), s32[]{:S(2)}) async-start(), calls=%async_computation.21 | async-start | bytes 5898240 | tf_op jit(solution)/shard_map/reduce_scatter | solution.py:292
  796.8 543.0 %all-reduce.3.cloned.1.call-start = ((), (), s32[]{:S(2)}) async-start(), calls=%async_computation.34 | async-start | bytes 147456 | tf_op jit(solution)/shard_map/psum | solution.py:330
  (106 other events, 1127.5 us)
Sparse Core Ops, SparseCore 0:
  13.2 26.7 all-gather.18
  42.8 46.7 all-gather.30
  91.7 23.7 all-gather.20
  118.2 41.0 all-gather.32
  165.9 31.7 reduce-scatter.12
  199.8 24.0 all-gather.26
  226.1 24.0 all-gather.22
  253.2 42.6 all-gather.34
  298.1 22.8 all-gather.24
  323.3 41.0 all-gather.36
  491.3 48.9 reduce-scatter.16
  542.7 33.0 reduce-scatter.14
  581.0 24.0 all-gather.28
  608.7 62.5 reduce-scatter.26
  674.4 61.5 reduce-scatter.24
  739.6 65.8 reduce-scatter.22
  808.8 65.7 reduce-scatter.20
  878.3 67.9 reduce-scatter.34
  950.2 67.9 reduce-scatter.32
  1022.0 68.0 reduce-scatter.30
  1094.0 68.0 reduce-scatter.28
  1164.8 46.8 reduce-scatter.18
  1219.3 120.4 all-reduce.2
where the time goes:
time: 1360 us; the launch traced here: 1350 us
  waiting for transfers between devices  658 us (48%)
  matrix products  267 us (20%)
  other arithmetic  140 us (10%)
  blocking collectives  136 us (10%)
  local copies, waits for them, and re-layouts  110 us (8%)
  loops' own time  24.1 us (2%)
  between operations  15.7 us (1%)
    reduce_scatter x2, waiting for transfers between devices, local(): lax.psum_scatter(up_grad, 'dp', scatter_dimension=0, tiled=True)  142 us
    reduce_scatter x2, waiting for transfers between devices, local(): lax.psum_scatter(down_grad, 'dp', scatter_dimension=0, tiled=True)  142 us
    psum x1, waiting for transfers between devices, local(): lax.psum((gain_stack, shift_stack, branch_stack, qkv_stack, up_stack), ('...  121 us
    reduce_scatter x2, waiting for transfers between devices, local(): lax.psum_scatter(jnp.concatenate([against(grad_mixed, qkv_full), against(...  88.6 us
    reduce_scatter x2, waiting for transfers between devices, local(): lax.psum_scatter(qkv_grad, 'dp', scatter_dimension=0, tiled=True)  71.8 us
    all_gather x2, blocking collectives, local(): lax.all_gather(w_qkv[which_layer], 'dp', axis=0, tiled=True)  70.1 us
    all_gather x2, blocking collectives, local(): lax.all_gather(w_out[which_layer], 'dp', axis=0, tiled=True)  66.3 us
    dot_general x12, matrix products, block_scores(): jnp.einsum('qhd,khd->hqk', query_block, key_heads, preferred_element_type...  61.7 us
  transfers between devices with their start and end apart: 23, of which 13 were waited for; matrix products, arithmetic and copies ran while one was open for 34% of the time, Pallas kernels for 0%

commit v1 on v0

v1 whole, which is shorter than its diff:
```python
import math

import jax
import jax.numpy as jnp
from jax import lax
from jax.experimental import pallas as pl
from jax.experimental.pallas import tpu as pltpu
from jax.sharding import PartitionSpec as P

D = 768
HEADS = 12
HEAD_DIM = 64
FF = 3072
ROT = 16
HALF = ROT // 2
LAYERS = 2
NORM_EPS = 1e-05
MASKED = -1e30
SCALE = HEAD_DIM ** (-0.5)
BF = jnp.bfloat16
F32 = jnp.float32


def dot(left, right, left_dim, right_dim):
    return lax.dot_general(
        left, right, (((left_dim,), (right_dim,)), ((), ())), preferred_element_type=F32
    )


def swap(values, axis, bit):
    count = lax.axis_size(axis)
    return lax.ppermute(values, axis, [(i, i ^ (1 << bit)) for i in range(count)])


def gather_rows(block, axis):
    count = lax.axis_size(axis)
    rank = lax.axis_index(axis)
    held = block[None]
    for bit in reversed(range(count.bit_length() - 1)):
        other = swap(held, axis, bit)
        first = ((rank >> bit) & 1) == 0
        held = jnp.stack(
            [jnp.where(first, held, other), jnp.where(first, other, held)], axis=1
        ).reshape((2 * held.shape[0],) + block.shape)
    return held.reshape((count * block.shape[0],) + block.shape[1:])


def scatter_rows(total, axis):
    count = lax.axis_size(axis)
    rank = lax.axis_index(axis)
    rows = total.shape[0] // count
    held = total.reshape((count, rows) + total.shape[1:])
    for bit in range(count.bit_length() - 1):
        mine = (rank >> bit) & 1
        pairs = held.reshape((held.shape[0] // 2, 2) + held.shape[1:])
        keep = lax.dynamic_index_in_dim(pairs, mine, axis=1, keepdims=False)
        send = lax.dynamic_index_in_dim(pairs, 1 - mine, axis=1, keepdims=False)
        held = keep + swap(send.astype(BF), axis, bit).astype(F32)
    return held[0]


def sum_over(values, axis):
    for bit in range(lax.axis_size(axis).bit_length() - 1):
        values = values + swap(values, axis, bit)
    return values


def segment_starts(seg_group):
    places = jnp.arange(seg_group.shape[0], dtype=jnp.int32)
    fresh = jnp.concatenate([jnp.ones((1,), dtype=bool), seg_group[1:] != seg_group[:-1]])
    return lax.cummax(jnp.where(fresh, places, 0), axis=0)


def turned(rows, cosine, sine):
    first, second = rows[:HALF], rows[HALF:ROT]
    return jnp.concatenate(
        [first * cosine - second * sine, second * cosine + first * sine, rows[ROT:]], axis=0
    )


def masked_scores(keys, queries, starts, first_query):
    scores = dot(keys, queries, 0, 0)
    key_place = lax.broadcasted_iota(jnp.int32, scores.shape, 0)
    query_place = lax.broadcasted_iota(jnp.int32, scores.shape, 1) + first_query
    allowed = (key_place <= query_place) & (key_place >= starts)
    return jnp.where(allowed, scores, MASKED)


def forward_kernel(block, mixed_ref, cos_ref, sin_ref, start_ref, qkv_ref, ctx_ref, log_ref):
    cosine, sine = cos_ref[...], sin_ref[...]
    queries = turned(mixed_ref[:HEAD_DIM], cosine, sine).astype(BF)
    keys = turned(mixed_ref[HEAD_DIM : 2 * HEAD_DIM], cosine, sine).astype(BF)
    values = mixed_ref[2 * HEAD_DIM :].astype(BF)
    qkv_ref[:HEAD_DIM] = queries
    qkv_ref[HEAD_DIM : 2 * HEAD_DIM] = keys
    qkv_ref[2 * HEAD_DIM :] = values
    for first in range(0, mixed_ref.shape[1], block):
        here = slice(first, first + block)
        seen = first + block
        scaled = queries[:, here] * jnp.asarray(SCALE, BF)
        scores = masked_scores(keys[:, :seen], scaled, start_ref[:, here], first)
        top = jnp.max(scores, axis=0, keepdims=True)
        weights = jnp.exp(scores - top)
        total = jnp.sum(weights, axis=0, keepdims=True)
        context = dot(values[:, :seen], weights.astype(BF), 1, 0)
        ctx_ref[:, here] = (context / total).astype(BF)
        log_ref[:, here] = jnp.broadcast_to(top + jnp.log(total), (8, block))


def backward_kernel(
    block, qkv_ref, grad_ref, log_ref, cos_ref, sin_ref, start_ref, out_ref, dq_ref, dk_ref, dv_ref
):
    dk_ref[...] = jnp.zeros_like(dk_ref)
    dv_ref[...] = jnp.zeros_like(dv_ref)
    for first in range(0, qkv_ref.shape[1], block):
        here = slice(first, first + block)
        seen = first + block
        scaled = qkv_ref[:HEAD_DIM, here] * jnp.asarray(SCALE, BF)
        keys = qkv_ref[HEAD_DIM : 2 * HEAD_DIM, :seen]
        values = qkv_ref[2 * HEAD_DIM :, :seen]
        grad = grad_ref[:, here]
        scores = masked_scores(keys, scaled, start_ref[:, here], first)
        prob = jnp.exp(scores - log_ref[:1, here])
        grad_prob = dot(values, grad, 0, 0)
        inner = jnp.sum(prob * grad_prob, axis=0, keepdims=True)
        grad_scores = (prob * (grad_prob - inner)).astype(BF)
        dv_ref[:, :seen] += dot(grad, prob.astype(BF), 1, 1)
        dk_ref[:, :seen] += dot(scaled, grad_scores, 1, 1)
        dq_ref[:, here] = dot(keys, grad_scores, 1, 0) * SCALE
    cosine, sine = cos_ref[...], sin_ref[...]
    out_ref[:HEAD_DIM] = turned(dq_ref[...], cosine, -sine).astype(BF)
    out_ref[HEAD_DIM : 2 * HEAD_DIM] = turned(dk_ref[...], cosine, -sine).astype(BF)
    out_ref[2 * HEAD_DIM :] = dv_ref[...].astype(BF)


def by_head(rows, tokens):
    return pl.BlockSpec((rows, tokens), lambda h: (h, 0))


def shared(rows, tokens):
    return pl.BlockSpec((rows, tokens), lambda h: (0, 0))


def attention_forward(mixed, cosine, sine, starts, heads):
    tokens = mixed.shape[1]
    block = min(512, tokens)
    return pl.pallas_call(
        lambda *refs: forward_kernel(block, *refs),
        grid=(heads,),
        in_specs=[
            by_head(3 * HEAD_DIM, tokens),
            shared(HALF, tokens),
            shared(HALF, tokens),
            shared(1, tokens),
        ],
        out_specs=[by_head(3 * HEAD_DIM, tokens), by_head(HEAD_DIM, tokens), by_head(8, tokens)],
        out_shape=[
            jax.ShapeDtypeStruct((heads * 3 * HEAD_DIM, tokens), BF),
            jax.ShapeDtypeStruct((heads * HEAD_DIM, tokens), BF),
            jax.ShapeDtypeStruct((heads * 8, tokens), F32),
        ],
        compiler_params=pltpu.CompilerParams(vmem_limit_bytes=48 * 2**20),
        cost_estimate=pl.CostEstimate(
            flops=10**10, bytes_accessed=8 * 10**6, transcendentals=heads * tokens * tokens
        ),
    )(mixed, cosine, sine, starts)


def attention_backward(qkv, grad_context, logsum, cosine, sine, starts, heads):
    tokens = qkv.shape[1]
    block = min(512, tokens)
    return pl.pallas_call(
        lambda *refs: backward_kernel(block, *refs),
        grid=(heads,),
        in_specs=[
            by_head(3 * HEAD_DIM, tokens),
            by_head(HEAD_DIM, tokens),
            by_head(8, tokens),
            shared(HALF, tokens),
            shared(HALF, tokens),
            shared(1, tokens),
        ],
        out_specs=by_head(3 * HEAD_DIM, tokens),
        out_shape=jax.ShapeDtypeStruct((heads * 3 * HEAD_DIM, tokens), BF),
        scratch_shapes=[pltpu.VMEM((HEAD_DIM, tokens), F32)] * 3,
        compiler_params=pltpu.CompilerParams(vmem_limit_bytes=48 * 2**20),
        cost_estimate=pl.CostEstimate(
            flops=25 * 10**9, bytes_accessed=8 * 10**6, transcendentals=heads * tokens * tokens
        ),
    )(qkv, grad_context, logsum, cosine, sine, starts)


def local(
    hidden,
    segments,
    w_qkv,
    w_out,
    w_up,
    w_down,
    ln_gain,
    ln_bias,
    branch_bias,
    qkv_bias,
    up_bias,
    cotangent,
):
    tensor_rank = lax.axis_index("tensor")
    tensor_count = lax.axis_size("tensor")
    local_heads = HEADS // tensor_count
    width_qkv = w_qkv.shape[2]
    width_up = w_up.shape[2]
    tokens = segments.shape[0]

    starts = segment_starts(segments)
    place = jnp.arange(tokens, dtype=jnp.int32) - starts
    exponent = jnp.arange(HALF, dtype=F32) * (-2.0 * math.log(10000.0) / ROT)
    angles = jnp.exp(exponent)[:, None] * place.astype(F32)[None, :]
    cosine, sine = jnp.cos(angles), jnp.sin(angles)
    starts = starts[None, :]

    weights = []
    for layer in range(LAYERS):
        into = gather_rows(jnp.concatenate([w_up[layer], w_qkv[layer]], axis=1), "dp")
        back = gather_rows(jnp.concatenate([w_down[layer], w_out[layer]], axis=1), "dp")
        weights.append((into[:, width_up:], back[:, width_up:], into[:, :width_up], back[:, :width_up]))

    stored = []
    for layer in range(LAYERS):
        qkv_full, out_full, up_full, down_full = weights[layer]
        average = jnp.mean(hidden, axis=-1, keepdims=True)
        centered = hidden - average
        variance = jnp.mean(centered * centered, axis=-1, keepdims=True)
        root = lax.rsqrt(variance + NORM_EPS)
        unit = centered * root
        unit_rows = gather_rows(unit.astype(BF), "tensor")
        wide = unit_rows.astype(F32)
        rows_one = (wide * ln_gain[layer, 0] + ln_bias[layer, 0]).astype(BF)
        rows_two = (wide * ln_gain[layer, 1] + ln_bias[layer, 1]).astype(BF)
        qkv_here = lax.dynamic_slice_in_dim(qkv_bias[layer], tensor_rank * width_qkv, width_qkv)
        mixed = dot(qkv_full, rows_one, 0, 1) + qkv_here[:, None]
        qkv, context, logsum = attention_forward(mixed, cosine, sine, starts, local_heads)
        up_here = lax.dynamic_slice_in_dim(up_bias[layer], tensor_rank * width_up, width_up)
        up_proj = dot(rows_two, up_full, 1, 0) + up_here
        activated = jax.nn.gelu(up_proj, approximate=False).astype(BF)
        branch = scatter_rows(
            dot(activated, down_full, 1, 1) + dot(context, out_full, 0, 1), "tensor"
        )
        stored.append((unit, root, unit_rows, qkv, context, logsum, up_proj, activated))
        hidden = hidden + branch + branch_bias[layer]

    grad_hidden = cotangent
    weight_parts = [None] * LAYERS
    small_parts = [None] * LAYERS
    inverse_root = 1.0 / math.sqrt(2.0)
    density = 1.0 / math.sqrt(2.0 * math.pi)
    for layer in reversed(range(LAYERS)):
        unit, root, unit_rows, qkv, context, logsum, up_proj, activated = stored[layer]
        qkv_full, out_full, up_full, down_full = weights[layer]
        gain_one, gain_two = ln_gain[layer, 0], ln_gain[layer, 1]
        shift_one, shift_two = ln_bias[layer, 0], ln_bias[layer, 1]
        grad_branch = grad_hidden.astype(BF)
        branch_sum = jnp.sum(grad_branch.astype(F32), axis=0)
        grad_rows = gather_rows(grad_branch, "tensor")

        grad_context = dot(out_full, grad_rows, 0, 1).astype(BF)
        grad_mixed = attention_backward(
            qkv, grad_context, logsum, cosine, sine, starts, local_heads
        )
        grad_act = dot(grad_rows, down_full, 1, 0)
        normal_cdf = 0.5 * (1.0 + lax.erf(up_proj * inverse_root))
        slope = normal_cdf + up_proj * jnp.exp(-0.5 * up_proj * up_proj) * density
        grad_up = (grad_act * slope).astype(BF)

        grad_unit = scatter_rows(
            dot(grad_mixed, qkv_full, 0, 1) * gain_one + dot(grad_up, up_full, 1, 1) * gain_two,
            "tensor",
        )
        pull = grad_unit - jnp.mean(grad_unit, axis=-1, keepdims=True)
        pull = pull - unit * jnp.mean(grad_unit * unit, axis=-1, keepdims=True)
        grad_hidden = grad_hidden + root * pull

        back_grad = jnp.concatenate(
            [dot(grad_rows, activated, 0, 0), dot(grad_rows, context, 0, 1)], axis=1
        )
        up_sum = jnp.sum(grad_up.astype(F32), axis=0)
        qkv_sum = jnp.sum(grad_mixed.astype(F32), axis=1)
        up_unit = dot(unit_rows, grad_up, 0, 0)
        qkv_unit = dot(unit_rows, grad_mixed, 0, 1)
        up_grad = up_unit * gain_two[:, None] + shift_two[:, None] * up_sum
        qkv_grad = qkv_unit * gain_one[:, None] + shift_one[:, None] * qkv_sum
        up_wide, qkv_wide = up_full.astype(F32), qkv_full.astype(F32)
        weight_parts[layer] = (
            scatter_rows(back_grad, "dp"),
            scatter_rows(up_grad, "dp"),
            scatter_rows(qkv_grad, "dp"),
        )
        small = jnp.concatenate(
            [
                jnp.sum(qkv_wide * qkv_unit, axis=1),
                jnp.sum(up_wide * up_unit, axis=1),
                jnp.sum(qkv_wide * qkv_sum, axis=1),
                jnp.sum(up_wide * up_sum, axis=1),
                branch_sum,
                up_sum,
                qkv_sum,
            ]
        )
        small_parts[layer] = gather_rows(sum_over(small, "dp")[None], "tensor")

    small_all = jnp.stack(small_parts)
    summed = jnp.sum(small_all[:, :, : 5 * D], axis=1).reshape(LAYERS, 5, D)
    up_total = small_all[:, :, 5 * D : 5 * D + width_up].reshape(LAYERS, FF)
    qkv_total = small_all[:, :, 5 * D + width_up :].reshape(LAYERS, 3 * D)
    back_all = jnp.stack([parts[0] for parts in weight_parts])
    return (
        hidden,
        grad_hidden,
        jnp.stack([parts[2] for parts in weight_parts]),
        back_all[:, :, width_up:],
        jnp.stack([parts[1] for parts in weight_parts]),
        back_all[:, :, :width_up],
        summed[:, 0:2],
        summed[:, 2:4],
        summed[:, 4],
        qkv_total,
        up_total,
    )


def solution(mesh):
    return jax.shard_map(
        local,
        mesh=mesh,
        in_specs=(
            P(("dp", "tensor"), None),
            P("dp"),
            P(None, "dp", "tensor"),
            P(None, "dp", "tensor"),
            P(None, "dp", "tensor"),
            P(None, "dp", "tensor"),
            P(),
            P(),
            P(),
            P(),
            P(),
            P(("dp", "tensor"), None),
        ),
        out_specs=(
            P(("dp", "tensor"), None),
            P(("dp", "tensor"), None),
            P(None, "dp", "tensor"),
            P(None, "dp", "tensor"),
            P(None, "dp", "tensor"),
            P(None, "dp", "tensor"),
            P(),
            P(),
            P(),
            P(),
            P(),
        ),
        check_vma=False,
    )
```

time: 1360 us -> 522 us (0.38)
  waiting for transfers between devices: 658 us -> 200 us
  matrix products: 267 us -> 83.1 us
  blocking collectives: 136 us -> 0 us
  other arithmetic: 140 us -> 51.3 us
  starting transfers between devices: 1.73 us -> 74.9 us
  local copies, waits for them, and re-layouts: 110 us -> 59.7 us
  Pallas kernels: 0 us -> 44.5 us
  loops' own time: 24.1 us -> 0 us
    reduce_scatter x12 -> x0, waiting for transfers between devices: 504 us -> none  [the longest x2 142 us: local(): lax.psum_scatter(up_grad, 'dp', scatter_dimension=0, tiled=True)]
    ppermute x0 -> x56, waiting for transfers between devices: none -> 200 us  [swap(): return lax.ppermute(values, axis, [(i, i ^ 1 << bit) for i in range(count)])]
    dot_general x66 -> x24, matrix products: 267 us -> 83.1 us  [dot(): lax.dot_general(left, right, (((left_dim,), (right_dim,)), ((), ())), pre...]
    all_gather x4 -> x0, blocking collectives: 136 us -> none  [the longest x2 70.1 us: local(): lax.all_gather(w_qkv[which_layer], 'dp', axis=0, tiled=True)]
    psum x1 -> x0, waiting for transfers between devices: 121 us -> none  [local(): lax.psum((gain_stack, shift_stack, branch_stack, qkv_stack, up_stack), ('...]
    ppermute x0 -> x56, starting transfers between devices: none -> 74.9 us  [swap(): return lax.ppermute(values, axis, [(i, i ^ 1 << bit) for i in range(count)])]
    convert_element_type x11 -> x1, other arithmetic: 63 us -> 0.08 us  [local(): angles = jnp.exp(exponent)[:, None] * place.astype(F32)[None, :]]
    dynamic_update_slice x16 -> x0, local copies, waits for them, and re-layouts: 54.6 us -> none  [the longest x12 54.2 us: attention_backward(): lax.scan(one_block, (zero_grad, zero_grad), (first_rows, logsum))]
  transfers between devices with their start and end apart: 23 -> 56, of which waited for: 13 -> 30; matrix products, arithmetic and copies ran while one was open for 34% -> 24% of each run, Pallas kernels for 0% -> 2%
where the time goes in v1:
time: 522 us; the launch traced here: 516 us
  waiting for transfers between devices  200 us (38%)
  matrix products  83.1 us (16%)
  starting transfers between devices  74.9 us (14%)
  local copies, waits for them, and re-layouts  59.7 us (11%)
  other arithmetic  51.3 us (10%)
  Pallas kernels  44.5 us (9%)
    ppermute x56, waiting for transfers between devices, swap(): return lax.ppermute(values, axis, [(i, i ^ 1 << bit) for i in range(count)])  200 us
    dot_general x24, matrix products, dot(): lax.dot_general(left, right, (((left_dim,), (right_dim,)), ((), ())), pre...  83.1 us
    ppermute x56, starting transfers between devices, swap(): return lax.ppermute(values, axis, [(i, i ^ 1 << bit) for i in range(count)])  74.9 us
    pallas_call x2, Pallas kernels, attention_backward(): pl.pallas_call(lambda *refs: backward_kernel(block, *refs), grid=(heads,)...  26.8 us
    unnamed x166, local copies, waits for them, and re-layouts  23.5 us
    pallas_call x2, Pallas kernels, attention_forward(): pl.pallas_call(lambda *refs: forward_kernel(block, *refs), grid=(heads,),...  17.7 us
    another operation x38, other arithmetic, gather_rows(): jnp.stack([jnp.where(first, held, other), jnp.where(first, other, held)],...  16 us
    convert_element_type x26, local copies, waits for them, and re-layouts, scatter_rows(): held = keep + swap(send.astype(BF), axis, bit).astype(F32)  14.1 us
  transfers between devices with their start and end apart: 56, of which 30 were waited for; matrix products, arithmetic and copies ran while one was open for 24% of the time, Pallas kernels for 2%

profile of v1, /device:TPU:0, one launch (start us, length us, event | category | flops | bytes accessed | tf_op | source)
XLA Modules:
  0.0 515.8 jit_solution(5200495013813959415)
XLA Ops:
  20.7 18.6 %collective-permute-done.5 = bf16[1,96,960]{2,1,0:T(8,128)(2,1)} collective-permute-done((bf16[1,96,960]{2,1,0:T(8,128)(2,1)}, bf16[1,96,960]{2,1,0:T(8,128)(2,1)}, u32[]{:S(2)}, u32[]{:S(2)}) %collective-permute-start.5) | collective-permute-done | bytes 184352 | tf_op jit(solution)/shard_map/ppermute | solution.py:32
  42.3 6.3 %collective-permute-done.15 = bf16[1,96,960]{2,1,0:T(8,128)(2,1)} collective-permute-done((bf16[1,96,960]{2,1,0:T(8,128)(2,1)}, bf16[1,96,960]{2,1,0:T(8,128)(2,1)}, u32[]{:S(2)}, u32[]{:S(2)}) %collective-permute-start.15) | collective-permute-done | bytes 184352 | tf_op jit(solution)/shard_map/ppermute | solution.py:32
  52.8 7.8 %collective-permute-done.6 = bf16[2,96,960]{2,1,0:T(8,128)(2,1)S(1)} collective-permute-done((bf16[2,96,960]{2,1,0:T(8,128)(2,1)S(1)}, bf16[2,96,960]{2,1,0:T(8,128)(2,1)S(1)}, u32[]{:S(2)}, u32[]{:S(2)}) %collective-permute-start.6) | collective-permute-done | bytes 368672 | tf_op jit(solution)/shard_map/ppermute | solution.py:32
  64.0 6.4 %collective-permute-done.3 = bf16[2,96,1344]{2,1,0:T(8,128)(2,1)S(1)} collective-permute-done((bf16[2,96,1344]{2,1,0:T(8,128)(2,1)S(1)}, bf16[2,96,1344]{2,1,0:T(8,128)(2,1)S(1)}, u32[]{:S(2)}, u32[]{:S(2)}) %collective-permute-start.3) | collective-permute-done | bytes 516128 | tf_op jit(solution)/shard_map/ppermute | solution.py:32
  72.8 8.5 %collective-permute-done.7 = bf16[4,96,960]{2,1,0:T(8,128)(2,1)S(1)} collective-permute-done((bf16[4,96,960]{2,1,0:T(8,128)(2,1)S(1)}, bf16[4,96,960]{2,1,0:T(8,128)(2,1)S(1)}, u32[]{:S(2)}, u32[]{:S(2)}) %collective-permute-start.7) | collective-permute-done | bytes 737312 | tf_op jit(solution)/shard_map/ppermute | solution.py:32
  83.0 17.1 %collective-permute-done.4 = bf16[4,96,1344]{2,1,0:T(8,128)(2,1)S(1)} collective-permute-done((bf16[4,96,1344]{2,1,0:T(8,128)(2,1)S(1)}, bf16[4,96,1344]{2,1,0:T(8,128)(2,1)S(1)}, u32[]{:S(2)}, u32[]{:S(2)}) %collective-permute-start.4) | collective-permute-done | bytes 1032224 | tf_op jit(solution)/shard_map/ppermute | solution.py:32
  100.8 13.3 %fusion.10 = (bf16[1536,768]{1,0:T(8,128)(2,1)S(1)}, f32[1536,768]{1,0:T(8,128)}) fusion(f32[768]{0:T(1024)S(1)} %get-tuple-element.145, bf16[768,1344]{1,0:T(8,128)(2,1)S(1)} %bitcast.462, bf16[1536,768]{1,0:T(8,128)(2,1)S(1)} %bitcast.502, f32[768]{0:T(1024)S(1)} %get-tuple-element.59, f32[768]{0:T(1024)S(1)} %get-tuple-element.148), kind=kOutput, calls=%fused_computation.18 | convolution fusion | flops 1894514688 | bytes 10629120 | tf_op jit(solution)/shard_map/dot_general | solution.py:25
  118.2 9.0 %shard_map.203 = (bf16[576,1536]{1,0:T(8,128)(2,1)S(1)}, bf16[192,1536]{1,0:T(8,128)(2,1)S(1)}, f32[24,1536]{1,0:T(8,128)S(1)}) custom-call(f32[576,1536]{1,0:T(8,128)S(1)} %convolution_add_fusion.3.refs_0_, f32[8,1536]{1,0:T(8,128)S(1)} %get-tuple-element.136.refs_1_.refs_3_, f32[8,1536]{1,0:T(8,128)S(1)} %get-tuple-element.135.refs_2_.refs_4_, ...), custom_call_target="tpu_custom_call" | custom-call | flops 10000000000 | bytes 8000000 | tf_op jit(solution)/shard_map/pallas_call | solution.py:147
  139.2 6.8 %collective-permute-done.13 = bf16[2,96,1344]{2,1,0:T(8,128)(2,1)S(1)} collective-permute-done((bf16[2,96,1344]{2,1,0:T(8,128)(2,1)S(1)}, bf16[2,96,1344]{2,1,0:T(8,128)(2,1)S(1)}, u32[]{:S(2)}, u32[]{:S(2)}) %collective-permute-start.13) | collective-permute-done | bytes 516128 | tf_op jit(solution)/shard_map/ppermute | solution.py:32
  147.9 6.8 %collective-permute-done.17 = bf16[4,96,960]{2,1,0:T(8,128)(2,1)S(1)} collective-permute-done((bf16[4,96,960]{2,1,0:T(8,128)(2,1)S(1)}, bf16[4,96,960]{2,1,0:T(8,128)(2,1)S(1)}, u32[]{:S(2)}, u32[]{:S(2)}) %collective-permute-start.17) | collective-permute-done | bytes 737312 | tf_op jit(solution)/shard_map/ppermute | solution.py:32
  158.0 11.7 %collective-permute-done.10 = bf16[1,384,768]{2,1,0:T(8,128)(2,1)S(1)} collective-permute-done((bf16[1,384,768]{2,1,0:T(8,128)(2,1)S(1)}, bf16[1,384,768]{2,1,0:T(8,128)(2,1)S(1)}, u32[]{:S(2)}, u32[]{:S(2)}) %collective-permute-start.10) | collective-permute-done | bytes 589856 | tf_op jit(solution)/shard_map/ppermute | solution.py:32
  190.2 8.7 %shard_map.204 = (bf16[576,1536]{1,0:T(8,128)(2,1)S(1)}, bf16[192,1536]{1,0:T(8,128)(2,1)S(1)}, f32[24,1536]{1,0:T(8,128)S(1)}) custom-call(f32[576,1536]{1,0:T(8,128)S(1)} %convolution_add_fusion.2.refs_0_, f32[8,1536]{1,0:T(8,128)S(1)} %get-tuple-element.136.refs_1_.refs_3_, f32[8,1536]{1,0:T(8,128)S(1)} %get-tuple-element.135.refs_2_.refs_4_, ...), custom_call_target="tpu_custom_call" | custom-call | flops 10000000000 | bytes 8000000 | tf_op jit(solution)/shard_map/pallas_call | solution.py:147
  199.0 13.3 %shard_map.205 = bf16[576,1536]{1,0:T(8,128)(2,1)S(1)} custom-call(bf16[576,1536]{1,0:T(8,128)(2,1)S(1)} %get-tuple-element.19.refs_0_, bf16[192,1536]{1,0:T(8,128)(2,1)S(1)} %convolution_convert_fusion.1.refs_1_, f32[24,1536]{1,0:T(8,128)S(1)} %get-tuple-element.20.refs_2_, f32[8,1536]{1,0:T(8,128)S(1)} %get-tuple-element.136.refs_1_.refs_3_, ...), custom_call_target="tpu_custom_call" | custom-call | flops 24999999488 | bytes 8000000 | tf_op jit(solution)/shard_map/pallas_call | solution.py:172
  214.7 12.0 %fusion.13 = (bf16[1536,768]{1,0:T(8,128)(2,1)S(1)}, f32[1536,768]{1,0:T(8,128)S(1)}) fusion(f32[768]{0:T(1024)S(1)} %get-tuple-element.146, bf16[768,1344]{1,0:T(8,128)(2,1)S(1)} %bitcast.471, bf16[1536,768]{1,0:T(8,128)(2,1)S(1)} %bitcast.507, f32[768]{0:T(1024)S(1)} %get-tuple-element.60, f32[768]{0:T(1024)S(1)} %get-tuple-element.147), kind=kOutput, calls=%fused_computation.21 | convolution fusion | flops 1894514688 | bytes 10629120 | tf_op jit(solution)/shard_map/dot_general | solution.py:25
  271.5 26.7 %collective-permute-done.31 = bf16[4,96,576]{2,1,0:T(8,128)(2,1)S(1)} collective-permute-done((bf16[4,96,576]{2,1,0:T(8,128)(2,1)S(1)}, bf16[4,96,576]{2,1,0:T(8,128)(2,1)S(1)}, u32[]{:S(2)}, u32[]{:S(2)}) %collective-permute-start.31) | collective-permute-done | bytes 442400 | tf_op jit(solution)/shard_map/ppermute | solution.py:32
  329.4 5.5 %collective-permute-done.23 = bf16[1,384,768]{2,1,0:T(8,128)(2,1)S(1)} collective-permute-done((bf16[1,384,768]{2,1,0:T(8,128)(2,1)S(1)}, bf16[1,384,768]{2,1,0:T(8,128)(2,1)S(1)}, u32[]{:S(2)}, u32[]{:S(2)}) %collective-permute-start.23) | collective-permute-done | bytes 589856 | tf_op jit(solution)/shard_map/ppermute | solution.py:32
  335.5 8.2 %collective-permute-done.19 = bf16[1,384,768]{2,1,0:T(8,128)(2,1)S(1)} collective-permute-done((bf16[1,384,768]{2,1,0:T(8,128)(2,1)S(1)}, bf16[1,384,768]{2,1,0:T(8,128)(2,1)S(1)}, u32[]{:S(2)}, u32[]{:S(2)}) %collective-permute-start.19) | collective-permute-done | bytes 589856 | tf_op jit(solution)/shard_map/ppermute | solution.py:32
  363.1 7.4 %collective-permute-done.24 = bf16[1,384,768]{2,1,0:T(8,128)(2,1)S(1)} collective-permute-done((bf16[1,384,768]{2,1,0:T(8,128)(2,1)S(1)}, bf16[1,384,768]{2,1,0:T(8,128)(2,1)S(1)}, u32[]{:S(2)}, u32[]{:S(2)}) %collective-permute-start.24) | collective-permute-done | bytes 589856 | tf_op jit(solution)/shard_map/ppermute | solution.py:32
  384.4 13.5 %shard_map.206 = bf16[576,1536]{1,0:T(8,128)(2,1)S(1)} custom-call(bf16[576,1536]{1,0:T(8,128)(2,1)S(1)} %copy-done.3, bf16[192,1536]{1,0:T(8,128)(2,1)S(1)} %convolution_convert_fusion.refs_1_, f32[24,1536]{1,0:T(8,128)S(1)} %get-tuple-element.22.refs_2_, f32[8,1536]{1,0:T(8,128)S(1)} %get-tuple-element.136.refs_1_.refs_3_, ...), custom_call_target="tpu_custom_call" | custom-call | flops 24999999488 | bytes 8000000 | tf_op jit(solution)/shard_map/pallas_call | solution.py:172
  402.5 5.3 %convert_reduce_fusion.1 = (f32[768]{0:T(1024)S(1)}, bf16[1536,768]{1,0:T(8,128)(2,1)S(1)}) fusion(f32[1536,768]{1,0:T(8,128)} %get-tuple-element.138, f32[768]{0:T(1024)S(1)} %copy-done.62, bf16[1536,768]{1,0:T(8,128)(2,1)S(1)} %bitcast.453, bf16[768,960]{1,0:T(8,128)(2,1)S(1)} %bitcast.483), kind=kOutput, calls=%fused_computation.35 | convolution fusion | flops 1827273984 | bytes 10624000 | tf_op jit(solution)/shard_map/dot_general | solution.py:25
  439.5 5.6 %multiply_add_fusion = f32[1536,768]{1,0:T(8,128)S(1)} fusion(f32[1536,768]{1,0:T(8,128)} %fusion.124, bf16[1536,768]{1,0:T(8,128)(2,1)} %copy-done.63, f32[768]{0:T(1024)S(1)} %copy-done.54, f32[768]{0:T(1024)S(1)} %copy-done.52, bf16[768,1344]{1,0:T(8,128)(2,1)} %bitcast.465), kind=kOutput, calls=%fused_computation.36 | convolution fusion | flops 1815478272 | bytes 12982272 | tf_op jit(solution)/shard_map/dot_general | solution.py:25
  453.4 13.6 %collective-permute-done.28 = bf16[4,96,576]{2,1,0:T(8,128)(2,1)} collective-permute-done((bf16[4,96,576]{2,1,0:T(8,128)(2,1)S(1)}, bf16[4,96,576]{2,1,0:T(8,128)(2,1)}, u32[]{:S(2)}, u32[]{:S(2)}) %collective-permute-start.28) | collective-permute-done | bytes 442400 | tf_op jit(solution)/shard_map/ppermute | solution.py:32
  472.6 5.4 %collective-permute-done.29 = bf16[2,96,576]{2,1,0:T(8,128)(2,1)S(1)} collective-permute-done((bf16[2,96,576]{2,1,0:T(8,128)(2,1)S(1)}, bf16[2,96,576]{2,1,0:T(8,128)(2,1)S(1)}, u32[]{:S(2)}, u32[]{:S(2)}) %collective-permute-start.29) | collective-permute-done | bytes 221216 | tf_op jit(solution)/shard_map/ppermute | solution.py:32
  490.1 6.0 %collective-permute-done.42 = bf16[1,96,768]{2,1,0:T(8,128)(2,1)S(1)} collective-permute-done((bf16[1,96,768]{2,1,0:T(8,128)(2,1)S(1)}, bf16[1,96,768]{2,1,0:T(8,128)(2,1)S(1)}, u32[]{:S(2)}, u32[]{:S(2)}) %collective-permute-start.42) | collective-permute-done | bytes 147488 | tf_op jit(solution)/shard_map/ppermute | solution.py:32
  (468 shorter events, 269.8 us)
Async XLA Ops:
  3.5 126.1 %collective-permute-start.12 = (bf16[1,96,1344]{2,1,0:T(8,128)(2,1)}, bf16[1,96,1344]{2,1,0:T(8,128)(2,1)}, u32[]{:S(2)}, u32[]{:S(2)}) collective-permute-start(bf16[1,96,1344]{2,1,0:T(8,128)(2,1)} %maximum_bitcast_fusion.9), channel_id=1, source_target_pairs={{0,16},{4,20},{8,24},{12,28},{16,0},{20,4},{24,8},{28,12},{1,17},{... | collective-permute-start | bytes 774152 | tf_op jit(solution)/shard_map/ppermute | solution.py:32
  10.0 29.3 %collective-permute-start.5 = (bf16[1,96,960]{2,1,0:T(8,128)(2,1)}, bf16[1,96,960]{2,1,0:T(8,128)(2,1)}, u32[]{:S(2)}, u32[]{:S(2)}) collective-permute-start(bf16[1,96,960]{2,1,0:T(8,128)(2,1)} %maximum_bitcast_fusion.10), channel_id=1, source_target_pairs={{0,16},{4,20},{8,24},{12,28},{16,0},{20,4},{24,8},{28,12},{1,17},{... | collective-permute-start | bytes 552968 | tf_op jit(solution)/shard_map/ppermute | solution.py:32
  10.8 39.5 %collective-permute-start.2 = (bf16[1,96,1344]{2,1,0:T(8,128)(2,1)}, bf16[1,96,1344]{2,1,0:T(8,128)(2,1)}, u32[]{:S(2)}, u32[]{:S(2)}) collective-permute-start(bf16[1,96,1344]{2,1,0:T(8,128)(2,1)} %maximum_bitcast_fusion.8), channel_id=1, source_target_pairs={{0,16},{4,20},{8,24},{12,28},{16,0},{20,4},{24,8},{28,12},{1,17},{... | collective-permute-start | bytes 774152 | tf_op jit(solution)/shard_map/ppermute | solution.py:32
  15.3 47.1 %collective-permute-start = (bf16[1,384,768]{2,1,0:T(8,128)(2,1)}, bf16[1,384,768]{2,1,0:T(8,128)(2,1)}, u32[]{:S(2)}, u32[]{:S(2)}) collective-permute-start(bf16[1,384,768]{2,1,0:T(8,128)(2,1)} %fusion.91), channel_id=1, source_target_pairs={{0,2},{1,3},{2,0},{3,1},{4,6},{5,7},{6,4},{7,5},{8,10},{9,11},{10,... | collective-permute-start | bytes 1769480 | tf_op jit(solution)/shard_map/ppermute | solution.py:32
  17.5 31.1 %collective-permute-start.15 = (bf16[1,96,960]{2,1,0:T(8,128)(2,1)}, bf16[1,96,960]{2,1,0:T(8,128)(2,1)}, u32[]{:S(2)}, u32[]{:S(2)}) collective-permute-start(bf16[1,96,960]{2,1,0:T(8,128)(2,1)} %maximum_bitcast_fusion.11), channel_id=1, source_target_pairs={{0,16},{4,20},{8,24},{12,28},{16,0},{20,4},{24,8},{28,12},{1,17},{... | collective-permute-start | bytes 552968 | tf_op jit(solution)/shard_map/ppermute | solution.py:32
  39.4 96.5 %collective-permute-start.20 = (bf16[1,384,768]{2,1,0:T(8,128)(2,1)}, bf16[1,384,768]{2,1,0:T(8,128)(2,1)}, u32[]{:S(2)}, u32[]{:S(2)}) collective-permute-start(bf16[1,384,768]{2,1,0:T(8,128)(2,1)} %convert_bitcast_fusion.1), channel_id=1, source_target_pairs={{0,2},{1,3},{2,0},{3,1},{4,6},{5,7},{6,4},{7,5},{8,10},{9,11},{10,... | collective-permute-start | bytes 1769480 | tf_op jit(solution)/shard_map/ppermute | solution.py:32
  51.4 19.0 %collective-permute-start.3 = (bf16[2,96,1344]{2,1,0:T(8,128)(2,1)S(1)}, bf16[2,96,1344]{2,1,0:T(8,128)(2,1)S(1)}, u32[]{:S(2)}, u32[]{:S(2)}) collective-permute-start(bf16[2,96,1344]{2,1,0:T(8,128)(2,1)S(1)} %maximum_bitcast_fusion.4), channel_id=1, source_target_pairs={{0,8},{4,12},{8,0},{12,4},{16,24},{20,28},{24,16},{28,20},{1,9},{5... | collective-permute-start | bytes 1548296 | tf_op jit(solution)/shard_map/ppermute | solution.py:32
  60.7 20.5 %collective-permute-start.7 = (bf16[4,96,960]{2,1,0:T(8,128)(2,1)S(1)}, bf16[4,96,960]{2,1,0:T(8,128)(2,1)S(1)}, u32[]{:S(2)}, u32[]{:S(2)}) collective-permute-start(bf16[4,96,960]{2,1,0:T(8,128)(2,1)S(1)} %bitcast.489), channel_id=1, source_target_pairs={{0,4},{4,0},{8,12},{12,8},{16,20},{20,16},{24,28},{28,24},{1,5},{5... | collective-permute-start | bytes 2211848 | tf_op jit(solution)/shard_map/ppermute | solution.py:32
  63.9 18.5 %collective-permute-start.1 = (bf16[2,384,768]{2,1,0:T(8,128)(2,1)S(1)}, bf16[2,384,768]{2,1,0:T(8,128)(2,1)S(1)}, u32[]{:S(2)}, u32[]{:S(2)}) collective-permute-start(bf16[2,384,768]{2,1,0:T(8,128)(2,1)S(1)} %maximum_bitcast_fusion), channel_id=1, source_target_pairs={{0,1},{1,0},{2,3},{3,2},{4,5},{5,4},{6,7},{7,6},{8,9},{9,8},{10,11... | collective-permute-start | bytes 3538952 | tf_op jit(solution)/shard_map/ppermute | solution.py:32
  70.7 29.3 %collective-permute-start.4 = (bf16[4,96,1344]{2,1,0:T(8,128)(2,1)S(1)}, bf16[4,96,1344]{2,1,0:T(8,128)(2,1)S(1)}, u32[]{:S(2)}, u32[]{:S(2)}) collective-permute-start(bf16[4,96,1344]{2,1,0:T(8,128)(2,1)S(1)} %bitcast.475), channel_id=1, source_target_pairs={{0,4},{4,0},{8,12},{12,8},{16,20},{20,16},{24,28},{28,24},{1,5},{5... | collective-permute-start | bytes 3096584 | tf_op jit(solution)/shard_map/ppermute | solution.py:32
  81.3 51.8 %collective-permute-start.16 = (bf16[2,96,960]{2,1,0:T(8,128)(2,1)}, bf16[2,96,960]{2,1,0:T(8,128)(2,1)}, u32[]{:S(2)}, u32[]{:S(2)}) collective-permute-start(bf16[2,96,960]{2,1,0:T(8,128)(2,1)} %maximum_bitcast_fusion.7), channel_id=1, source_target_pairs={{0,8},{4,12},{8,0},{12,4},{16,24},{20,28},{24,16},{28,20},{1,9},{5... | collective-permute-start | bytes 1105928 | tf_op jit(solution)/shard_map/ppermute | solution.py:32
  134.3 20.4 %collective-permute-start.17 = (bf16[4,96,960]{2,1,0:T(8,128)(2,1)S(1)}, bf16[4,96,960]{2,1,0:T(8,128)(2,1)S(1)}, u32[]{:S(2)}, u32[]{:S(2)}) collective-permute-start(bf16[4,96,960]{2,1,0:T(8,128)(2,1)S(1)} %bitcast.488), channel_id=1, source_target_pairs={{0,4},{4,0},{8,12},{12,8},{16,20},{20,16},{24,28},{28,24},{1,5},{5... | collective-permute-start | bytes 2211848 | tf_op jit(solution)/shard_map/ppermute | solution.py:32
  137.2 20.4 %collective-permute-start.21 = (bf16[2,384,768]{2,1,0:T(8,128)(2,1)S(1)}, bf16[2,384,768]{2,1,0:T(8,128)(2,1)S(1)}, u32[]{:S(2)}, u32[]{:S(2)}) collective-permute-start(bf16[2,384,768]{2,1,0:T(8,128)(2,1)S(1)} %maximum_bitcast_fusion.2), channel_id=1, source_target_pairs={{0,1},{1,0},{2,3},{3,2},{4,5},{5,4},{6,7},{7,6},{8,9},{9,8},{10,11... | collective-permute-start | bytes 3538952 | tf_op jit(solution)/shard_map/ppermute | solution.py:32
  146.3 30.8 %collective-permute-start.14 = (bf16[4,96,1344]{2,1,0:T(8,128)(2,1)S(1)}, bf16[4,96,1344]{2,1,0:T(8,128)(2,1)S(1)}, u32[]{:S(2)}, u32[]{:S(2)}) collective-permute-start(bf16[4,96,1344]{2,1,0:T(8,128)(2,1)S(1)} %bitcast.474), channel_id=1, source_target_pairs={{0,4},{4,0},{8,12},{12,8},{16,20},{20,16},{24,28},{28,24},{1,5},{5... | collective-permute-start | bytes 3096584 | tf_op jit(solution)/shard_map/ppermute | solution.py:32
  237.6 88.5 %collective-permute-start.18 = (bf16[2,384,768]{2,1,0:T(8,128)(2,1)}, bf16[2,384,768]{2,1,0:T(8,128)(2,1)}, u32[]{:S(2)}, u32[]{:S(2)}) collective-permute-start(bf16[2,384,768]{2,1,0:T(8,128)(2,1)} %fusion.64), channel_id=1, source_target_pairs={{0,1},{1,0},{2,3},{3,2},{4,5},{5,4},{6,7},{7,6},{8,9},{9,8},{10,11... | collective-permute-start | bytes 3538952 | tf_op jit(solution)/shard_map/ppermute | solution.py:32
  247.1 72.4 %collective-permute-start.22 = (bf16[2,384,768]{2,1,0:T(8,128)(2,1)}, bf16[2,384,768]{2,1,0:T(8,128)(2,1)}, u32[]{:S(2)}, u32[]{:S(2)}) collective-permute-start(bf16[2,384,768]{2,1,0:T(8,128)(2,1)} %fusion.63), channel_id=1, source_target_pairs={{0,1},{1,0},{2,3},{3,2},{4,5},{5,4},{6,7},{7,6},{8,9},{9,8},{10,11... | collective-permute-start | bytes 3538952 | tf_op jit(solution)/shard_map/ppermute | solution.py:32
  255.4 55.5 %collective-permute-start.37 = (bf16[4,96,960]{2,1,0:T(8,128)(2,1)}, bf16[4,96,960]{2,1,0:T(8,128)(2,1)}, u32[]{:S(2)}, u32[]{:S(2)}) collective-permute-start(bf16[4,96,960]{2,1,0:T(8,128)(2,1)} %fusion.85), channel_id=1, source_target_pairs={{0,4},{4,0},{8,12},{12,8},{16,20},{20,16},{24,28},{28,24},{1,5},{5... | collective-permute-start | bytes 2211848 | tf_op jit(solution)/shard_map/ppermute | solution.py:32
  259.1 39.7 %collective-permute-start.43 = (bf16[4,96,768]{2,1,0:T(8,128)(2,1)}, bf16[4,96,768]{2,1,0:T(8,128)(2,1)}, u32[]{:S(2)}, u32[]{:S(2)}) collective-permute-start(bf16[4,96,768]{2,1,0:T(8,128)(2,1)} %fusion.93), channel_id=1, source_target_pairs={{0,4},{4,0},{8,12},{12,8},{16,20},{20,16},{24,28},{28,24},{1,5},{5... | collective-permute-start | bytes 1769480 | tf_op jit(solution)/shard_map/ppermute | solution.py:32
  264.8 33.5 %collective-permute-start.31 = (bf16[4,96,576]{2,1,0:T(8,128)(2,1)S(1)}, bf16[4,96,576]{2,1,0:T(8,128)(2,1)S(1)}, u32[]{:S(2)}, u32[]{:S(2)}) collective-permute-start(bf16[4,96,576]{2,1,0:T(8,128)(2,1)S(1)} %fusion.95), channel_id=1, source_target_pairs={{0,4},{4,0},{8,12},{12,8},{16,20},{20,16},{24,28},{28,24},{1,5},{5... | collective-permute-start | bytes 1327112 | tf_op jit(solution)/shard_map/ppermute | solution.py:32
  318.0 34.3 %collective-permute-start.45 = (bf16[1,96,768]{2,1,0:T(8,128)(2,1)S(1)}, bf16[1,96,768]{2,1,0:T(8,128)(2,1)S(1)}, u32[]{:S(2)}, u32[]{:S(2)}) collective-permute-start(bf16[1,96,768]{2,1,0:T(8,128)(2,1)S(1)} %dynamic-slice_convert_fusion.15), channel_id=1, source_target_pairs={{0,16},{4,20},{8,24},{12,28},{16,0},{20,4},{24,8},{28,12},{1,17},{... | collective-permute-start | bytes 442376 | tf_op jit(solution)/shard_map/ppermute | solution.py:32
  424.2 56.8 %collective-permute-start.34 = (bf16[4,96,960]{2,1,0:T(8,128)(2,1)}, bf16[4,96,960]{2,1,0:T(8,128)(2,1)}, u32[]{:S(2)}, u32[]{:S(2)}) collective-permute-start(bf16[4,96,960]{2,1,0:T(8,128)(2,1)} %fusion.84), channel_id=1, source_target_pairs={{0,4},{4,0},{8,12},{12,8},{16,20},{20,16},{24,28},{28,24},{1,5},{5... | collective-permute-start | bytes 2211848 | tf_op jit(solution)/shard_map/ppermute | solution.py:32
  429.6 41.5 %collective-permute-start.40 = (bf16[4,96,768]{2,1,0:T(8,128)(2,1)S(1)}, bf16[4,96,768]{2,1,0:T(8,128)(2,1)}, u32[]{:S(2)}, u32[]{:S(2)}) collective-permute-start(bf16[4,96,768]{2,1,0:T(8,128)(2,1)S(1)} %fusion.92), channel_id=1, source_target_pairs={{0,4},{4,0},{8,12},{12,8},{16,20},{20,16},{24,28},{28,24},{1,5},{5... | collective-permute-start | bytes 1769480 | tf_op jit(solution)/shard_map/ppermute | solution.py:32
  437.3 29.8 %collective-permute-start.28 = (bf16[4,96,576]{2,1,0:T(8,128)(2,1)S(1)}, bf16[4,96,576]{2,1,0:T(8,128)(2,1)}, u32[]{:S(2)}, u32[]{:S(2)}) collective-permute-start(bf16[4,96,576]{2,1,0:T(8,128)(2,1)S(1)} %fusion.94), channel_id=1, source_target_pairs={{0,4},{4,0},{8,12},{12,8},{16,20},{20,16},{24,28},{28,24},{1,5},{5... | collective-permute-start | bytes 1327112 | tf_op jit(solution)/shard_map/ppermute | solution.py:32
  448.4 51.4 %collective-permute-start.26 = (bf16[2,384,768]{2,1,0:T(8,128)(2,1)}, bf16[2,384,768]{2,1,0:T(8,128)(2,1)}, u32[]{:S(2)}, u32[]{:S(2)}) collective-permute-start(bf16[2,384,768]{2,1,0:T(8,128)(2,1)} %fusion.65), channel_id=1, source_target_pairs={{0,1},{1,0},{2,3},{3,2},{4,5},{5,4},{6,7},{7,6},{8,9},{9,8},{10,11... | collective-permute-start | bytes 3538952 | tf_op jit(solution)/shard_map/ppermute | solution.py:32
  (104 other events, 1610.2 us)

commit v2 on v1

--- a/solution.py
+++ b/solution.py
@@ -32,31 +32,69 @@
     return lax.ppermute(values, axis, [(i, i ^ (1 << bit)) for i in range(count)])
 
 
-def gather_rows(block, axis):
+def after(values, *markers):
+    return lax.optimization_barrier((values,) + markers)[0]
+
+
+def gather_steps(block, axis, turns=None):
     count = lax.axis_size(axis)
     rank = lax.axis_index(axis)
     held = block[None]
+    arrived = []
+    joined = None
     for bit in reversed(range(count.bit_length() - 1)):
+        if joined is not None:
+            held = joined()
+        way = min(bit, 1)
+        if turns is not None and way in turns:
+            held = after(held, turns[way])
         other = swap(held, axis, bit)
-        first = ((rank >> bit) & 1) == 0
-        held = jnp.stack(
-            [jnp.where(first, held, other), jnp.where(first, other, held)], axis=1
-        ).reshape((2 * held.shape[0],) + block.shape)
-    return held.reshape((count * block.shape[0],) + block.shape[1:])
-
-
-def scatter_rows(total, axis):
+        if turns is not None:
+            turns[way] = other
+        arrived.append(other)
+
+        def joined(*markers, held=held, other=other, bit=bit):
+            if markers:
+                other = after(other, *markers)
+            first = ((rank >> bit) & 1) == 0
+            return jnp.stack(
+                [jnp.where(first, held, other), jnp.where(first, other, held)], axis=1
+            ).reshape((2 * held.shape[0],) + block.shape)
+
+    def finish(*markers):
+        whole = block[None] if joined is None else joined(*markers)
+        return whole.reshape((count * block.shape[0],) + block.shape[1:])
+
+    return finish, arrived
+
+
+def gather_rows(block, axis):
+    return gather_steps(block, axis)[0]()
+
+
+def scatter_rows(totals, axis, waits=(), arrived=None):
     count = lax.axis_size(axis)
     rank = lax.axis_index(axis)
-    rows = total.shape[0] // count
-    held = total.reshape((count, rows) + total.shape[1:])
+    held = [total.reshape((count, total.shape[0] // count, total.shape[1])) for total in totals]
     for bit in range(count.bit_length() - 1):
         mine = (rank >> bit) & 1
-        pairs = held.reshape((held.shape[0] // 2, 2) + held.shape[1:])
-        keep = lax.dynamic_index_in_dim(pairs, mine, axis=1, keepdims=False)
-        send = lax.dynamic_index_in_dim(pairs, 1 - mine, axis=1, keepdims=False)
-        held = keep + swap(send.astype(BF), axis, bit).astype(F32)
-    return held[0]
+        pairs = [part.reshape((part.shape[0] // 2, 2) + part.shape[1:]) for part in held]
+        keep = [lax.dynamic_index_in_dim(part, mine, axis=1, keepdims=False) for part in pairs]
+        send = [
+            lax.dynamic_index_in_dim(part, 1 - mine, axis=1, keepdims=False).astype(BF)
+            for part in pairs
+        ]
+        other = swap(send[0] if len(send) == 1 else jnp.concatenate(send, axis=2), axis, bit)
+        if arrived is not None:
+            arrived.append(other)
+        if bit < len(waits):
+            other = after(other, waits[bit])
+        held, begin = [], 0
+        for part in keep:
+            end = begin + part.shape[2]
+            held.append(part + other[:, :, begin:end].astype(F32))
+            begin = end
+    return [part[0] for part in held]
 
 
 def sum_over(values, axis):
@@ -219,14 +257,21 @@
     starts = starts[None, :]
 
     weights = []
+    steps = []
+    turns = {}
     for layer in range(LAYERS):
-        into = gather_rows(jnp.concatenate([w_up[layer], w_qkv[layer]], axis=1), "dp")
-        back = gather_rows(jnp.concatenate([w_down[layer], w_out[layer]], axis=1), "dp")
-        weights.append((into[:, width_up:], back[:, width_up:], into[:, :width_up], back[:, :width_up]))
+        into = gather_steps(jnp.concatenate([w_up[layer], w_qkv[layer]], axis=1), "dp", turns)
+        back = gather_steps(jnp.concatenate([w_down[layer], w_out[layer]], axis=1), "dp", turns)
+        steps.append((into, back))
 
     stored = []
+    inverse_root = 1.0 / math.sqrt(2.0)
+    density = 1.0 / math.sqrt(2.0 * math.pi)
     for layer in range(LAYERS):
-        qkv_full, out_full, up_full, down_full = weights[layer]
+        (into_end, into_arrived), (back_end, back_arrived) = steps[layer]
+        coming = steps[layer + 1][0][1] if layer + 1 < LAYERS else []
+        into = into_end()
+        up_full, qkv_full = into[:, :width_up], into[:, width_up:]
         average = jnp.mean(hidden, axis=-1, keepdims=True)
         centered = hidden - average
         variance = jnp.mean(centered * centered, axis=-1, keepdims=True)
@@ -238,23 +283,35 @@
         rows_two = (wide * ln_gain[layer, 1] + ln_bias[layer, 1]).astype(BF)
         qkv_here = lax.dynamic_slice_in_dim(qkv_bias[layer], tensor_rank * width_qkv, width_qkv)
         mixed = dot(qkv_full, rows_one, 0, 1) + qkv_here[:, None]
+        if coming:
+            mixed = after(mixed, coming[0])
         qkv, context, logsum = attention_forward(mixed, cosine, sine, starts, local_heads)
         up_here = lax.dynamic_slice_in_dim(up_bias[layer], tensor_rank * width_up, width_up)
         up_proj = dot(rows_two, up_full, 1, 0) + up_here
-        activated = jax.nn.gelu(up_proj, approximate=False).astype(BF)
-        branch = scatter_rows(
-            dot(activated, down_full, 1, 1) + dot(context, out_full, 0, 1), "tensor"
+        up_proj, normal_cdf = lax.optimization_barrier(
+            (up_proj, 0.5 * (1.0 + lax.erf(up_proj * inverse_root)))
         )
-        stored.append((unit, root, unit_rows, qkv, context, logsum, up_proj, activated))
+        activated = (up_proj * normal_cdf).astype(BF)
+        back = back_end(context)
+        down_full, out_full = back[:, :width_up], back[:, width_up:]
+        weights.append((qkv_full, out_full, up_full, down_full))
+        if len(coming) > 1:
+            context = after(context, coming[1])
+        arrived = []
+        (branch,) = scatter_rows(
+            [dot(activated, down_full, 1, 1) + dot(context, out_full, 0, 1)],
+            "tensor",
+            arrived=arrived,
+        )
+        stored.append((unit, root, unit_rows, qkv, context, logsum, up_proj, normal_cdf, activated))
         hidden = hidden + branch + branch_bias[layer]
 
     grad_hidden = cotangent
     weight_parts = [None] * LAYERS
     small_parts = [None] * LAYERS
-    inverse_root = 1.0 / math.sqrt(2.0)
-    density = 1.0 / math.sqrt(2.0 * math.pi)
+    waiting = None
     for layer in reversed(range(LAYERS)):
-        unit, root, unit_rows, qkv, context, logsum, up_proj, activated = stored[layer]
+        unit, root, unit_rows, qkv, context, logsum, up_proj, normal_cdf, activated = stored[layer]
         qkv_full, out_full, up_full, down_full = weights[layer]
         gain_one, gain_two = ln_gain[layer, 0], ln_gain[layer, 1]
         shift_one, shift_two = ln_bias[layer, 0], ln_bias[layer, 1]
@@ -262,39 +319,73 @@
         branch_sum = jnp.sum(grad_branch.astype(F32), axis=0)
         grad_rows = gather_rows(grad_branch, "tensor")
 
+        def back_grads(rows):
+            return [dot(rows, activated, 0, 0), dot(rows, context, 0, 1)]
+
+        def up_grads(pulled):
+            total = jnp.sum(pulled.astype(F32), axis=0)
+            product = dot(unit_rows, pulled, 0, 0)
+            return total, product, product * gain_two[:, None] + shift_two[:, None] * total
+
+        if layer == LAYERS - 1 and arrived:
+            grad_rows = after(grad_rows, arrived[0])
+        back_grad = back_grads(grad_rows)
         grad_context = dot(out_full, grad_rows, 0, 1).astype(BF)
+        grad_act = dot(grad_rows, down_full, 1, 0)
+        slope = normal_cdf + up_proj * jnp.exp(-0.5 * up_proj * up_proj) * density
+        grad_up = (grad_act * slope).astype(BF)
+        if layer == 0:
+            up_sum, up_unit, up_grad = up_grads(grad_up)
+            grad_context = after(grad_context, up_grad, *back_grad)
+        else:
+            grad_context = after(grad_context, *back_grad)
+        received = []
+        if waiting is not None:
+            weight_parts[layer + 1], received = waiting(grad_rows, grad_context)
+        if received:
+            grad_context = after(grad_context, *received[0])
         grad_mixed = attention_backward(
             qkv, grad_context, logsum, cosine, sine, starts, local_heads
         )
-        grad_act = dot(grad_rows, down_full, 1, 0)
-        normal_cdf = 0.5 * (1.0 + lax.erf(up_proj * inverse_root))
-        slope = normal_cdf + up_proj * jnp.exp(-0.5 * up_proj * up_proj) * density
-        grad_up = (grad_act * slope).astype(BF)
-
-        grad_unit = scatter_rows(
-            dot(grad_mixed, qkv_full, 0, 1) * gain_one + dot(grad_up, up_full, 1, 1) * gain_two,
-            "tensor",
+        if len(received) > 1:
+            grad_up = after(grad_up, *received[1])
+        if layer == LAYERS - 1 and len(arrived) > 1:
+            grad_up = after(grad_up, arrived[-1])
+        unit_part = (
+            dot(grad_mixed, qkv_full, 0, 1) * gain_one + dot(grad_up, up_full, 1, 1) * gain_two
         )
+        if layer > 0:
+            up_sum, up_unit, up_grad = up_grads(after(grad_up, unit_part))
+            late_mixed = after(grad_mixed, unit_part)
+        else:
+            late_mixed = grad_mixed
+        (grad_unit,) = scatter_rows([unit_part], "tensor")
         pull = grad_unit - jnp.mean(grad_unit, axis=-1, keepdims=True)
         pull = pull - unit * jnp.mean(grad_unit * unit, axis=-1, keepdims=True)
         grad_hidden = grad_hidden + root * pull
 
-        back_grad = jnp.concatenate(
-            [dot(grad_rows, activated, 0, 0), dot(grad_rows, context, 0, 1)], axis=1
-        )
-        up_sum = jnp.sum(grad_up.astype(F32), axis=0)
-        qkv_sum = jnp.sum(grad_mixed.astype(F32), axis=1)
-        up_unit = dot(unit_rows, grad_up, 0, 0)
-        qkv_unit = dot(unit_rows, grad_mixed, 0, 1)
-        up_grad = up_unit * gain_two[:, None] + shift_two[:, None] * up_sum
+        qkv_sum = jnp.sum(late_mixed.astype(F32), axis=1)
+        qkv_unit = dot(unit_rows, late_mixed, 0, 1)
         qkv_grad = qkv_unit * gain_one[:, None] + shift_one[:, None] * qkv_sum
+
+        def sent(
+            *markers, back_grad=back_grad, up_grad=up_grad, qkv_grad=qkv_grad, unit_part=unit_part
+        ):
+            early = (unit_part,) + markers if markers else ()
+            up_arrived, qkv_arrived = [], []
+            parts = (
+                scatter_rows(back_grad, "dp", early)
+                + scatter_rows([up_grad], "dp", markers, up_arrived)
+                + scatter_rows([qkv_grad], "dp", markers, qkv_arrived)
+            )
+            return parts, list(zip(up_arrived, qkv_arrived))
+
+        if layer > 0:
+            waiting = sent
+        else:
+            weight_parts[layer] = sent()[0]
         up_wide, qkv_wide = up_full.astype(F32), qkv_full.astype(F32)
-        weight_parts[layer] = (
-            scatter_rows(back_grad, "dp"),
-            scatter_rows(up_grad, "dp"),
-            scatter_rows(qkv_grad, "dp"),
-        )
-        small = jnp.concatenate(
+        small_parts[layer] = jnp.concatenate(
             [
                 jnp.sum(qkv_wide * qkv_unit, axis=1),
                 jnp.sum(up_wide * up_unit, axis=1),
@@ -305,20 +396,19 @@
                 qkv_sum,
             ]
         )
-        small_parts[layer] = gather_rows(sum_over(small, "dp")[None], "tensor")
-
-    small_all = jnp.stack(small_parts)
+
+    small_all = gather_rows(sum_over(jnp.concatenate(small_parts), "dp")[None], "tensor")
+    small_all = small_all.reshape(tensor_count, LAYERS, -1).transpose(1, 0, 2)
     summed = jnp.sum(small_all[:, :, : 5 * D], axis=1).reshape(LAYERS, 5, D)
     up_total = small_all[:, :, 5 * D : 5 * D + width_up].reshape(LAYERS, FF)
     qkv_total = small_all[:, :, 5 * D + width_up :].reshape(LAYERS, 3 * D)
-    back_all = jnp.stack([parts[0] for parts in weight_parts])
     return (
         hidden,
         grad_hidden,
+        jnp.stack([parts[3] for parts in weight_parts]),
+        jnp.stack([parts[1] for parts in weight_parts]),
         jnp.stack([parts[2] for parts in weight_parts]),
-        back_all[:, :, width_up:],
-        jnp.stack([parts[1] for parts in weight_parts]),
-        back_all[:, :, :width_up],
+        jnp.stack([parts[0] for parts in weight_parts]),
         summed[:, 0:2],
         summed[:, 2:4],
         summed[:, 4],

time: 522 us -> 452 us (0.87)
  waiting for transfers between devices: 200 us -> 153 us
  starting transfers between devices: 74.9 us -> 59.1 us
  matrix products: 83.1 us -> 67.6 us
  other arithmetic: 51.3 us -> 58.3 us
    ppermute x56 -> x51, waiting for transfers between devices: 200 us -> 153 us  [swap(): return lax.ppermute(values, axis, [(i, i ^ 1 << bit) for i in range(count)])]
    ppermute x56 -> x51, starting transfers between devices: 74.9 us -> 59.1 us  [swap(): return lax.ppermute(values, axis, [(i, i ^ 1 << bit) for i in range(count)])]
    dot_general x24, matrix products: 83.1 us -> 67.6 us  [dot(): lax.dot_general(left, right, (((left_dim,), (right_dim,)), ((), ())), pre...]
    dynamic_slice x0 -> x6, local copies, waits for them, and re-layouts: none -> 8.4 us  [the longest x4 6.17 us: scatter_rows(): lax.dynamic_index_in_dim(part, mine, axis=1, keepdims=False)]
    concatenate x4 -> x1, local copies, waits for them, and re-layouts: 7.32 us -> 0.09 us  [local(): jnp.concatenate(small_parts)]
    unnamed x166 -> x175, local copies, waits for them, and re-layouts: 23.5 us -> 16.4 us
    add x22 -> x28, other arithmetic: 12.6 us -> 19 us  [scatter_rows(): held.append(part + other[:, :, begin:end].astype(F32))]
    another operation x41 -> x39, other arithmetic: 17.2 us -> 13.5 us  [the longest x35 11.5 us: joined(): jnp.stack([jnp.where(first, held, other), jnp.where(first, other, held)],...]
  transfers between devices with their start and end apart: 56 -> 51, of which waited for: 30 -> 26; matrix products, arithmetic and copies ran while one was open for 24% -> 31% of each run, Pallas kernels for 2% -> 7%
where the time goes in v2:
time: 452 us; the launch traced here: 443 us
  waiting for transfers between devices  153 us (34%)
  matrix products  67.6 us (15%)
  starting transfers between devices  59.1 us (13%)
  other arithmetic  58.3 us (13%)
  local copies, waits for them, and re-layouts  56.6 us (13%)
  Pallas kernels  44.7 us (10%)
    ppermute x51, waiting for transfers between devices, swap(): return lax.ppermute(values, axis, [(i, i ^ 1 << bit) for i in range(count)])  153 us
    dot_general x24, matrix products, dot(): lax.dot_general(left, right, (((left_dim,), (right_dim,)), ((), ())), pre...  67.6 us
    ppermute x51, starting transfers between devices, swap(): return lax.ppermute(values, axis, [(i, i ^ 1 << bit) for i in range(count)])  59.1 us
    pallas_call x2, Pallas kernels, attention_backward(): pl.pallas_call(lambda *refs: backward_kernel(block, *refs), grid=(heads,)...  27.2 us
    add x28, other arithmetic, scatter_rows(): held.append(part + other[:, :, begin:end].astype(F32))  19 us
    pallas_call x2, Pallas kernels, attention_forward(): pl.pallas_call(lambda *refs: forward_kernel(block, *refs), grid=(heads,),...  17.5 us
    unnamed x175, local copies, waits for them, and re-layouts  16.4 us
    convert_element_type x30, local copies, waits for them, and re-layouts, scatter_rows(): lax.dynamic_index_in_dim(part, 1 - mine, axis=1, keepdims=False).astype(BF)  13.9 us
  transfers between devices with their start and end apart: 51, of which 26 were waited for; matrix products, arithmetic and copies ran while one was open for 31% of the time, Pallas kernels for 7%

profile of v2, /device:TPU:0, one launch (start us, length us, event | category | flops | bytes accessed | tf_op | source)
XLA Modules:
  0.0 442.8 jit_solution(9452090069884442181)
XLA Ops:
  16.4 5.0 %collective-permute-done.2 = bf16[1,96,1344]{2,1,0:T(8,128)(2,1)} collective-permute-done((bf16[1,96,1344]{2,1,0:T(8,128)(2,1)}, bf16[1,96,1344]{2,1,0:T(8,128)(2,1)}, u32[]{:S(2)}, u32[]{:S(2)}) %collective-permute-start.2) | collective-permute-done | bytes 258080 | tf_op jit(solution)/shard_map/ppermute | solution.py:32
  24.3 11.8 %collective-permute-done.3 = bf16[2,96,1344]{2,1,0:T(8,128)(2,1)S(1)} collective-permute-done((bf16[2,96,1344]{2,1,0:T(8,128)(2,1)S(1)}, bf16[2,96,1344]{2,1,0:T(8,128)(2,1)S(1)}, u32[]{:S(2)}, u32[]{:S(2)}) %collective-permute-start.3) | collective-permute-done | bytes 516128 | tf_op jit(solution)/shard_map/ppermute | solution.py:32
  39.7 8.2 %collective-permute-done.5 = bf16[1,96,960]{2,1,0:T(8,128)(2,1)S(1)} collective-permute-done((bf16[1,96,960]{2,1,0:T(8,128)(2,1)S(1)}, bf16[1,96,960]{2,1,0:T(8,128)(2,1)S(1)}, u32[]{:S(2)}, u32[]{:S(2)}) %collective-permute-start.5) | collective-permute-done | bytes 184352 | tf_op jit(solution)/shard_map/ppermute | solution.py:32
  50.6 7.6 %collective-permute-done.6 = bf16[2,96,960]{2,1,0:T(8,128)(2,1)S(1)} collective-permute-done((bf16[2,96,960]{2,1,0:T(8,128)(2,1)S(1)}, bf16[2,96,960]{2,1,0:T(8,128)(2,1)S(1)}, u32[]{:S(2)}, u32[]{:S(2)}) %collective-permute-start.6) | collective-permute-done | bytes 368672 | tf_op jit(solution)/shard_map/ppermute | solution.py:32
  61.5 11.7 %collective-permute-done.8 = bf16[1,96,1344]{2,1,0:T(8,128)(2,1)S(1)} collective-permute-done((bf16[1,96,1344]{2,1,0:T(8,128)(2,1)S(1)}, bf16[1,96,1344]{2,1,0:T(8,128)(2,1)S(1)}, u32[]{:S(2)}, u32[]{:S(2)}) %collective-permute-start.8) | collective-permute-done | bytes 258080 | tf_op jit(solution)/shard_map/ppermute | solution.py:32
  83.4 8.7 %shard_map.203 = (bf16[576,1536]{1,0:T(8,128)(2,1)S(1)}, bf16[192,1536]{1,0:T(8,128)(2,1)S(1)}, f32[24,1536]{1,0:T(8,128)S(1)}) custom-call(f32[576,1536]{1,0:T(8,128)S(1)} %convolution_add_fusion.5.refs_0_, f32[8,1536]{1,0:T(8,128)S(1)} %get-tuple-element.209.refs_1_.refs_3_, f32[8,1536]{1,0:T(8,128)S(1)} %get-tuple-element.208.refs_2_.refs_4_, ...), custom_call_target="tpu_custom_call" | custom-call | flops 10000000000 | bytes 8000000 | tf_op jit(solution)/shard_map/pallas_call | solution.py:185
  106.8 13.7 %collective-permute-done.20 = bf16[1,384,768]{2,1,0:T(8,128)(2,1)} collective-permute-done((bf16[1,384,768]{2,1,0:T(8,128)(2,1)}, bf16[1,384,768]{2,1,0:T(8,128)(2,1)}, u32[]{:S(2)}, u32[]{:S(2)}) %collective-permute-start.20) | collective-permute-done | bytes 589856 | tf_op jit(solution)/shard_map/ppermute | solution.py:32
  131.3 7.8 %collective-permute-done.11 = bf16[1,384,768]{2,1,0:T(8,128)(2,1)S(1)} collective-permute-done((bf16[1,384,768]{2,1,0:T(8,128)(2,1)S(1)}, bf16[1,384,768]{2,1,0:T(8,128)(2,1)S(1)}, u32[]{:S(2)}, u32[]{:S(2)}) %collective-permute-start.11) | collective-permute-done | bytes 589856 | tf_op jit(solution)/shard_map/ppermute | solution.py:32
  143.8 10.3 %collective-permute-done.12 = bf16[1,384,768]{2,1,0:T(8,128)(2,1)S(1)} collective-permute-done((bf16[1,384,768]{2,1,0:T(8,128)(2,1)S(1)}, bf16[1,384,768]{2,1,0:T(8,128)(2,1)S(1)}, u32[]{:S(2)}, u32[]{:S(2)}) %collective-permute-start.12) | collective-permute-done | bytes 589856 | tf_op jit(solution)/shard_map/ppermute | solution.py:32
  154.8 11.3 %collective-permute-done.14 = bf16[4,96,1344]{2,1,0:T(8,128)(2,1)S(1)} collective-permute-done((bf16[4,96,1344]{2,1,0:T(8,128)(2,1)S(1)}, bf16[4,96,1344]{2,1,0:T(8,128)(2,1)S(1)}, u32[]{:S(2)}, u32[]{:S(2)}) %collective-permute-start.14) | collective-permute-done | bytes 1032224 | tf_op jit(solution)/shard_map/ppermute | solution.py:32
  170.4 8.8 %shard_map.204 = (bf16[576,1536]{1,0:T(8,128)(2,1)S(1)}, bf16[192,1536]{1,0:T(8,128)(2,1)S(1)}, f32[24,1536]{1,0:T(8,128)S(1)}) custom-call(f32[576,1536]{1,0:T(8,128)S(1)} %convolution_add_fusion.4.refs_0_, f32[8,1536]{1,0:T(8,128)S(1)} %get-tuple-element.209.refs_1_.refs_3_, f32[8,1536]{1,0:T(8,128)S(1)} %get-tuple-element.208.refs_2_.refs_4_, ...), custom_call_target="tpu_custom_call" | custom-call | flops 10000000000 | bytes 8000000 | tf_op jit(solution)/shard_map/pallas_call | solution.py:185
  203.7 13.7 %shard_map.205 = bf16[576,1536]{1,0:T(8,128)(2,1)S(1)} custom-call(bf16[576,1536]{1,0:T(8,128)(2,1)S(1)} %get-tuple-element.70.refs_0_, bf16[192,1536]{1,0:T(8,128)(2,1)S(1)} %convolution_convert_fusion.1.refs_1_, f32[24,1536]{1,0:T(8,128)S(1)} %get-tuple-element.73.refs_2_, f32[8,1536]{1,0:T(8,128)S(1)} %get-tuple-element.209.refs_1_.refs_3_, ...), custom_call_target="tpu_custom_call" | custom-call | flops 24999999488 | bytes 8000000 | tf_op jit(solution)/shard_map/pallas_call | solution.py:210
  217.4 6.6 %fusion.13 = bf16[1536,768]{1,0:T(8,128)(2,1)S(1)} fusion(f32[1536,768]{1,0:T(8,128)} %copy-done.20, f32[1536,768]{1,0:T(8,128)} %copy-done.21, bf16[1536,768]{1,0:T(8,128)(2,1)S(1)} %bitcast.440, bf16[768,960]{1,0:T(8,128)(2,1)S(1)} %bitcast.475), kind=kOutput, calls=%fused_computation.19 | convolution fusion | flops 1820196864 | bytes 15335424 | tf_op jit(solution)/shard_map/dot_general | solution.py:25
  249.6 5.4 %collective-permute-done.23 = bf16[1,384,768]{2,1,0:T(8,128)(2,1)S(1)} collective-permute-done((bf16[1,384,768]{2,1,0:T(8,128)(2,1)}, bf16[1,384,768]{2,1,0:T(8,128)(2,1)S(1)}, u32[]{:S(2)}, u32[]{:S(2)}) %collective-permute-start.23) | collective-permute-done | bytes 589856 | tf_op jit(solution)/shard_map/ppermute | solution.py:32
  266.1 8.7 %collective-permute-done.24 = bf16[1,384,768]{2,1,0:T(8,128)(2,1)S(1)} collective-permute-done((bf16[1,384,768]{2,1,0:T(8,128)(2,1)S(1)}, bf16[1,384,768]{2,1,0:T(8,128)(2,1)S(1)}, u32[]{:S(2)}, u32[]{:S(2)}) %collective-permute-start.24) | collective-permute-done | bytes 589856 | tf_op jit(solution)/shard_map/ppermute | solution.py:32
  296.0 6.7 %fusion.21 = (f32[768]{0:T(1024)S(1)}, f32[768]{0:T(1024)S(1)}, f32[768,768]{1,0:T(8,128)}) fusion(f32[768]{0:T(1024)S(1)} %get-tuple-element.214, bf16[768,1344]{1,0:T(8,128)(2,1)} %bitcast.498, f32[768]{0:T(1024)S(1)} %copy-done.75, f32[768]{0:T(1024)S(1)} %copy-done.69, bf16[1536,768]{1,0:T(8,128)(2,1)} %bitcast.490, bf16[1536,768]{1,0:T(8,128)(2,1)} %get-tuple-element.83), kind=kOutput, calls=%fused_computation.53 | convolution fusion | flops 1816656384 | bytes 8272896 | tf_op jit(solution)/shard_map/dot_general | solution.py:25
  309.7 13.6 %shard_map.206 = bf16[576,1536]{1,0:T(8,128)(2,1)S(1)} custom-call(bf16[576,1536]{1,0:T(8,128)(2,1)S(1)} %copy-done.1, bf16[192,1536]{1,0:T(8,128)(2,1)S(1)} %convolution_convert_fusion.refs_1_, f32[24,1536]{1,0:T(8,128)S(1)} %get-tuple-element.80.refs_2_, f32[8,1536]{1,0:T(8,128)S(1)} %get-tuple-element.209.refs_1_.refs_3_, ...), custom_call_target="tpu_custom_call" | custom-call | flops 24999999488 | bytes 8000000 | tf_op jit(solution)/shard_map/pallas_call | solution.py:210
  323.6 4.2 fusion.69
  384.2 5.7 %multiply_add_fusion = f32[1536,768]{1,0:T(8,128)S(1)} fusion(f32[1536,768]{1,0:T(8,128)} %fusion.69, bf16[1536,768]{1,0:T(8,128)(2,1)} %get-tuple-element.83, f32[768]{0:T(1024)S(1)} %copy-done.71, f32[768]{0:T(1024)S(1)} %copy-done.69, bf16[768,1344]{1,0:T(8,128)(2,1)} %bitcast.499), kind=kOutput, calls=%fused_computation.26 | convolution fusion | flops 1815478272 | bytes 12982272 | tf_op jit(solution)/shard_map/dot_general | solution.py:25
  398.0 5.5 %collective-permute-done.33 = bf16[2,96,576]{2,1,0:T(8,128)(2,1)S(1)} collective-permute-done((bf16[2,96,576]{2,1,0:T(8,128)(2,1)S(1)}, bf16[2,96,576]{2,1,0:T(8,128)(2,1)S(1)}, u32[]{:S(2)}, u32[]{:S(2)}) %collective-permute-start.33) | collective-permute-done | bytes 221216 | tf_op jit(solution)/shard_map/ppermute | solution.py:32
  408.1 4.3 collective-permute-done.43
  413.4 7.4 %collective-permute-done.44 = bf16[1,96,768]{2,1,0:T(8,128)(2,1)S(1)} collective-permute-done((bf16[1,96,768]{2,1,0:T(8,128)(2,1)S(1)}, bf16[1,96,768]{2,1,0:T(8,128)(2,1)S(1)}, u32[]{:S(2)}, u32[]{:S(2)}) %collective-permute-start.44) | collective-permute-done | bytes 147488 | tf_op jit(solution)/shard_map/ppermute | solution.py:32
  427.3 7.1 %collective-permute-done.38 = bf16[1,96,960]{2,1,0:T(8,128)(2,1)S(1)} collective-permute-done((bf16[1,96,960]{2,1,0:T(8,128)(2,1)S(1)}, bf16[1,96,960]{2,1,0:T(8,128)(2,1)S(1)}, u32[]{:S(2)}, u32[]{:S(2)}) %collective-permute-start.38) | collective-permute-done | bytes 184352 | tf_op jit(solution)/shard_map/ppermute | solution.py:32
  436.1 4.2 collective-permute-done.31
  (477 shorter events, 241.8 us)
Async XLA Ops:
  4.8 16.6 %collective-permute-start.2 = (bf16[1,96,1344]{2,1,0:T(8,128)(2,1)}, bf16[1,96,1344]{2,1,0:T(8,128)(2,1)}, u32[]{:S(2)}, u32[]{:S(2)}) collective-permute-start(bf16[1,96,1344]{2,1,0:T(8,128)(2,1)} %maximum_bitcast_fusion.8), channel_id=1, source_target_pairs={{0,16},{4,20},{8,24},{12,28},{16,0},{20,4},{24,8},{28,12},{1,17},{... | collective-permute-start | bytes 774152 | tf_op jit(solution)/shard_map/ppermute | solution.py:32
  9.5 29.7 %collective-permute-start = (bf16[1,384,768]{2,1,0:T(8,128)(2,1)S(1)}, bf16[1,384,768]{2,1,0:T(8,128)(2,1)S(1)}, u32[]{:S(2)}, u32[]{:S(2)}) collective-permute-start(bf16[1,384,768]{2,1,0:T(8,128)(2,1)S(1)} %fusion.73), channel_id=1, source_target_pairs={{0,2},{1,3},{2,0},{3,1},{4,6},{5,7},{6,4},{7,5},{8,10},{9,11},{10,... | collective-permute-start | bytes 1769480 | tf_op jit(solution)/shard_map/ppermute | solution.py:32
  39.6 34.5 %collective-permute-start.1 = (bf16[2,384,768]{2,1,0:T(8,128)(2,1)S(1)}, bf16[2,384,768]{2,1,0:T(8,128)(2,1)S(1)}, u32[]{:S(2)}, u32[]{:S(2)}) collective-permute-start(bf16[2,384,768]{2,1,0:T(8,128)(2,1)S(1)} %maximum_bitcast_fusion), channel_id=1, source_target_pairs={{0,1},{1,0},{2,3},{3,2},{4,5},{5,4},{6,7},{7,6},{8,9},{9,8},{10,11... | collective-permute-start | bytes 3538952 | tf_op jit(solution)/shard_map/ppermute | solution.py:32
  49.0 25.7 %collective-permute-start.4 = (bf16[4,96,1344]{2,1,0:T(8,128)(2,1)S(1)}, bf16[4,96,1344]{2,1,0:T(8,128)(2,1)S(1)}, u32[]{:S(2)}, u32[]{:S(2)}) collective-permute-start(bf16[4,96,1344]{2,1,0:T(8,128)(2,1)S(1)} %bitcast.457), channel_id=1, source_target_pairs={{0,4},{4,0},{8,12},{12,8},{16,20},{20,16},{24,28},{28,24},{1,5},{5... | collective-permute-start | bytes 3096584 | tf_op jit(solution)/shard_map/ppermute | solution.py:32
  73.4 22.5 %collective-permute-start.9 = (bf16[2,96,1344]{2,1,0:T(8,128)(2,1)S(1)}, bf16[2,96,1344]{2,1,0:T(8,128)(2,1)}, u32[]{:S(2)}, u32[]{:S(2)}) collective-permute-start(bf16[2,96,1344]{2,1,0:T(8,128)(2,1)S(1)} %maximum_bitcast_fusion.5), channel_id=1, source_target_pairs={{0,8},{4,12},{8,0},{12,4},{16,24},{20,28},{24,16},{28,20},{1,9},{5... | collective-permute-start | bytes 1548296 | tf_op jit(solution)/shard_map/ppermute | solution.py:32
  74.7 21.2 %collective-permute-start.7 = (bf16[4,96,960]{2,1,0:T(8,128)(2,1)S(1)}, bf16[4,96,960]{2,1,0:T(8,128)(2,1)S(1)}, u32[]{:S(2)}, u32[]{:S(2)}) collective-permute-start(bf16[4,96,960]{2,1,0:T(8,128)(2,1)S(1)} %bitcast.476), channel_id=1, source_target_pairs={{0,4},{4,0},{8,12},{12,8},{16,20},{20,16},{24,28},{28,24},{1,5},{5... | collective-permute-start | bytes 2211848 | tf_op jit(solution)/shard_map/ppermute | solution.py:32
  103.6 18.1 %collective-permute-start.10 = (bf16[2,384,768]{2,1,0:T(8,128)(2,1)}, bf16[2,384,768]{2,1,0:T(8,128)(2,1)}, u32[]{:S(2)}, u32[]{:S(2)}) collective-permute-start(bf16[2,384,768]{2,1,0:T(8,128)(2,1)} %fusion.40), channel_id=1, source_target_pairs={{0,1},{1,0},{2,3},{3,2},{4,5},{5,4},{6,7},{7,6},{8,9},{9,8},{10,11... | collective-permute-start | bytes 3538952 | tf_op jit(solution)/shard_map/ppermute | solution.py:32
  126.8 68.0 %collective-permute-start.21 = (bf16[2,384,768]{2,1,0:T(8,128)(2,1)}, bf16[2,384,768]{2,1,0:T(8,128)(2,1)}, u32[]{:S(2)}, u32[]{:S(2)}) collective-permute-start(bf16[2,384,768]{2,1,0:T(8,128)(2,1)} %maximum_bitcast_fusion.2), channel_id=1, source_target_pairs={{0,1},{1,0},{2,3},{3,2},{4,5},{5,4},{6,7},{7,6},{8,9},{9,8},{10,11... | collective-permute-start | bytes 3538952 | tf_op jit(solution)/shard_map/ppermute | solution.py:32
  141.7 24.4 %collective-permute-start.14 = (bf16[4,96,1344]{2,1,0:T(8,128)(2,1)S(1)}, bf16[4,96,1344]{2,1,0:T(8,128)(2,1)S(1)}, u32[]{:S(2)}, u32[]{:S(2)}) collective-permute-start(bf16[4,96,1344]{2,1,0:T(8,128)(2,1)S(1)} %bitcast.458), channel_id=1, source_target_pairs={{0,4},{4,0},{8,12},{12,8},{16,20},{20,16},{24,28},{28,24},{1,5},{5... | collective-permute-start | bytes 3096584 | tf_op jit(solution)/shard_map/ppermute | solution.py:32
  166.1 17.2 %collective-permute-start.17 = (bf16[4,96,960]{2,1,0:T(8,128)(2,1)S(1)}, bf16[4,96,960]{2,1,0:T(8,128)(2,1)}, u32[]{:S(2)}, u32[]{:S(2)}) collective-permute-start(bf16[4,96,960]{2,1,0:T(8,128)(2,1)S(1)} %bitcast.478), channel_id=1, source_target_pairs={{0,4},{4,0},{8,12},{12,8},{16,20},{20,16},{24,28},{28,24},{1,5},{5... | collective-permute-start | bytes 2211848 | tf_op jit(solution)/shard_map/ppermute | solution.py:32
  203.1 23.0 %collective-permute-start.19 = (bf16[1,384,768]{2,1,0:T(8,128)(2,1)S(1)}, bf16[1,384,768]{2,1,0:T(8,128)(2,1)S(1)}, u32[]{:S(2)}, u32[]{:S(2)}) collective-permute-start(bf16[1,384,768]{2,1,0:T(8,128)(2,1)S(1)} %dynamic-slice_convert_fusion.2), channel_id=1, source_target_pairs={{0,2},{1,3},{2,0},{3,1},{4,6},{5,7},{6,4},{7,5},{8,10},{9,11},{10,... | collective-permute-start | bytes 1769480 | tf_op jit(solution)/shard_map/ppermute | solution.py:32
  245.8 33.4 %collective-permute-start.39 = (bf16[4,96,960]{2,1,0:T(8,128)(2,1)}, bf16[4,96,960]{2,1,0:T(8,128)(2,1)}, u32[]{:S(2)}, u32[]{:S(2)}) collective-permute-start(bf16[4,96,960]{2,1,0:T(8,128)(2,1)} %pad_maximum_fusion.13), channel_id=1, source_target_pairs={{0,4},{4,0},{8,12},{12,8},{16,20},{20,16},{24,28},{28,24},{1,5},{5... | collective-permute-start | bytes 2211848 | tf_op jit(solution)/shard_map/ppermute | solution.py:32
  265.2 44.4 %collective-permute-start.27 = (bf16[4,96,576]{2,1,0:T(8,128)(2,1)}, bf16[4,96,576]{2,1,0:T(8,128)(2,1)}, u32[]{:S(2)}, u32[]{:S(2)}) collective-permute-start(bf16[4,96,576]{2,1,0:T(8,128)(2,1)} %fusion.78), channel_id=1, source_target_pairs={{0,4},{4,0},{8,12},{12,8},{16,20},{20,16},{24,28},{28,24},{1,5},{5... | collective-permute-start | bytes 1327112 | tf_op jit(solution)/shard_map/ppermute | solution.py:32
  278.8 30.9 %collective-permute-start.26 = (bf16[4,96,768]{2,1,0:T(8,128)(2,1)}, bf16[4,96,768]{2,1,0:T(8,128)(2,1)}, u32[]{:S(2)}, u32[]{:S(2)}) collective-permute-start(bf16[4,96,768]{2,1,0:T(8,128)(2,1)} %fusion.74), channel_id=1, source_target_pairs={{0,4},{4,0},{8,12},{12,8},{16,20},{20,16},{24,28},{28,24},{1,5},{5... | collective-permute-start | bytes 1769480 | tf_op jit(solution)/shard_map/ppermute | solution.py:32
  283.0 22.9 %collective-permute-start.40 = (bf16[2,96,960]{2,1,0:T(8,128)(2,1)}, bf16[2,96,960]{2,1,0:T(8,128)(2,1)}, u32[]{:S(2)}, u32[]{:S(2)}) collective-permute-start(bf16[2,96,960]{2,1,0:T(8,128)(2,1)} %pad_maximum_fusion.18), channel_id=1, source_target_pairs={{0,8},{4,12},{8,0},{12,4},{16,24},{20,28},{24,16},{28,20},{1,9},{5... | collective-permute-start | bytes 1105928 | tf_op jit(solution)/shard_map/ppermute | solution.py:32
  331.8 16.9 %collective-permute-start.46 = (f32[10368]{0:T(1024)S(1)}, f32[10368]{0:T(1024)S(1)}, u32[]{:S(2)}, u32[]{:S(2)}) collective-permute-start(f32[10368]{0:T(1024)S(1)} %concatenate.50), channel_id=1, source_target_pairs={{0,4},{4,0},{8,12},{12,8},{16,20},{20,16},{24,28},{28,24},{1,5},{5... | collective-permute-start | bytes 124424 | tf_op jit(solution)/shard_map/ppermute | solution.py:32
  335.2 69.4 %collective-permute-start.36 = (bf16[4,96,960]{2,1,0:T(8,128)(2,1)}, bf16[4,96,960]{2,1,0:T(8,128)(2,1)}, u32[]{:S(2)}, u32[]{:S(2)}) collective-permute-start(bf16[4,96,960]{2,1,0:T(8,128)(2,1)} %pad_maximum_fusion.12), channel_id=1, source_target_pairs={{0,4},{4,0},{8,12},{12,8},{16,20},{20,16},{24,28},{28,24},{1,5},{5... | collective-permute-start | bytes 2211848 | tf_op jit(solution)/shard_map/ppermute | solution.py:32
  339.4 24.3 %collective-permute-start.41 = (bf16[1,96,960]{2,1,0:T(8,128)(2,1)S(1)}, bf16[1,96,960]{2,1,0:T(8,128)(2,1)S(1)}, u32[]{:S(2)}, u32[]{:S(2)}) collective-permute-start(bf16[1,96,960]{2,1,0:T(8,128)(2,1)S(1)} %pad_maximum_fusion.20), channel_id=1, source_target_pairs={{0,16},{4,20},{8,24},{12,28},{16,0},{20,4},{24,8},{28,12},{1,17},{... | collective-permute-start | bytes 552968 | tf_op jit(solution)/shard_map/ppermute | solution.py:32
  344.2 50.5 %collective-permute-start.42 = (bf16[4,96,768]{2,1,0:T(8,128)(2,1)}, bf16[4,96,768]{2,1,0:T(8,128)(2,1)}, u32[]{:S(2)}, u32[]{:S(2)}) collective-permute-start(bf16[4,96,768]{2,1,0:T(8,128)(2,1)} %fusion.76), channel_id=1, source_target_pairs={{0,4},{4,0},{8,12},{12,8},{16,20},{20,16},{24,28},{28,24},{1,5},{5... | collective-permute-start | bytes 1769480 | tf_op jit(solution)/shard_map/ppermute | solution.py:32
  351.0 31.9 %collective-permute-start.28 = (bf16[2,96,768]{2,1,0:T(8,128)(2,1)}, bf16[2,96,768]{2,1,0:T(8,128)(2,1)}, u32[]{:S(2)}, u32[]{:S(2)}) collective-permute-start(bf16[2,96,768]{2,1,0:T(8,128)(2,1)} %fusion.86), channel_id=1, source_target_pairs={{0,8},{4,12},{8,0},{12,4},{16,24},{20,28},{24,16},{28,20},{1,9},{5... | collective-permute-start | bytes 884744 | tf_op jit(solution)/shard_map/ppermute | solution.py:32
  362.7 30.7 %collective-permute-start.32 = (bf16[4,96,576]{2,1,0:T(8,128)(2,1)}, bf16[4,96,576]{2,1,0:T(8,128)(2,1)}, u32[]{:S(2)}, u32[]{:S(2)}) collective-permute-start(bf16[4,96,576]{2,1,0:T(8,128)(2,1)} %fusion.79), channel_id=1, source_target_pairs={{0,4},{4,0},{8,12},{12,8},{16,20},{20,16},{24,28},{28,24},{1,5},{5... | collective-permute-start | bytes 1327112 | tf_op jit(solution)/shard_map/ppermute | solution.py:32
  371.2 18.9 %collective-permute-start.35 = (bf16[1,96,576]{2,1,0:T(8,128)(2,1)}, bf16[1,96,576]{2,1,0:T(8,128)(2,1)S(1)}, u32[]{:S(2)}, u32[]{:S(2)}) collective-permute-start(bf16[1,96,576]{2,1,0:T(8,128)(2,1)} %dynamic-slice_convert_fusion.11), channel_id=1, source_target_pairs={{0,16},{4,20},{8,24},{12,28},{16,0},{20,4},{24,8},{28,12},{1,17},{... | collective-permute-start | bytes 331784 | tf_op jit(solution)/shard_map/ppermute | solution.py:32
  390.1 35.3 %collective-permute-start.30 = (bf16[2,384,768]{2,1,0:T(8,128)(2,1)S(1)}, bf16[2,384,768]{2,1,0:T(8,128)(2,1)S(1)}, u32[]{:S(2)}, u32[]{:S(2)}) collective-permute-start(bf16[2,384,768]{2,1,0:T(8,128)(2,1)S(1)} %fusion.43), channel_id=1, source_target_pairs={{0,1},{1,0},{2,3},{3,2},{4,5},{5,4},{6,7},{7,6},{8,9},{9,8},{10,11... | collective-permute-start | bytes 3538952 | tf_op jit(solution)/shard_map/ppermute | solution.py:32
  395.9 16.5 %collective-permute-start.43 = (bf16[2,96,768]{2,1,0:T(8,128)(2,1)S(1)}, bf16[2,96,768]{2,1,0:T(8,128)(2,1)S(1)}, u32[]{:S(2)}, u32[]{:S(2)}) collective-permute-start(bf16[2,96,768]{2,1,0:T(8,128)(2,1)S(1)} %fusion.89), channel_id=1, source_target_pairs={{0,8},{4,12},{8,0},{12,4},{16,24},{20,28},{24,16},{28,20},{1,9},{5... | collective-permute-start | bytes 884744 | tf_op jit(solution)/shard_map/ppermute | solution.py:32
  (112 other events, 825.8 us)
